TPU v7x, 128 devices: a whole 4x4x4 slice. The times are simulated.
128 devices in a mesh: gx: 8 (over y, core), gy: 16 (over x, z).
Axes of the slice: x: 4, y: 4, z: 4, core: 2. Of those that a mesh axis runs over, the one named last changes fastest.
Arguments:
- adjoint_start: float32 [2, 1024, 4096], P(None, 'gx', 'gy'), may hold values from -4 to 4
- velocity: float32 [2, 1024, 4096], P(None, 'gx', 'gy'), may hold values from -6 to 6
- viscosity: float32 [1024, 4096], P('gx', 'gy'), may hold values from 0.1 to 1
- friction: float32 [1024, 4096], P('gx', 'gy'), may hold values from 0.1 to 2
- ice_mask: int32 [1024, 4096], P('gx', 'gy'), may hold values 0 or 1
- misfit: float32 [65536, 128], P(('gx', 'gy')), may hold values from -6 to 6
- heading: float32 [65536], P(('gx', 'gy')), may hold values from -3.140625 to 3.140625
- row_dest: int32 [65536, 1], P(('gx', 'gy')), may hold values from 0 to 127; in each aligned block of 512 rows (0 to 511, 512 to 1023, ...) at most 8 rows name the same one
- live_rows: int32 [128], P(('gx', 'gy')), may hold values from 384 to 512
- pixel_lists: int32 [16384, 8, 2, 128], P(('gx', 'gy')), may hold values from 0 to 255, as said below
Outputs:
- adjoint: float32 [2, 1024, 4096], P(None, 'gx', 'gy')
- friction_gradient: float32 [1024, 4096], P('gx', 'gy')
Inputs may be any that keep to these rules, and one draw needn't show every extreme that they name: `row_dest`: among the 512 rows of one device no tile is named more than 8 times. `pixel_lists`: entry 0 is a local row below 128, entry 1 a local column below 256.
All inputs are finite; a program needn't handle non-finite values. No bound on the sum of `ice_mask` on one device may be relied on, other than what follows from the above.
Results may differ from a plain program's by a relative error of at most 0.0003.
Values sent between devices are 32-bit elements; how exact they have to be, the bound alone decides.
A program may use at most 64 MiB of HBM per device.

v0:
```python
import math

import jax
import jax.numpy as jnp
from jax import lax
from jax.sharding import PartitionSpec as P

ITERS = 4


tau_step = 0.04


def extended(cells, sides, width):
    for axis, dim in sides:
        count = lax.axis_size(axis)
        ends = count - 1
        head = lax.slice_in_dim(cells, 0, width, axis=dim)
        tail = lax.slice_in_dim(cells, cells.shape[dim] - width, cells.shape[dim], axis=dim)
        cells = jnp.concatenate(
            [
                lax.ppermute(tail, axis, [(i, (i + 1) % count) for i in range(ends)]),
                cells,
                lax.ppermute(head, axis, [((i + 1) % count, i) for i in range(ends)]),
            ],
            axis=dim,
        )
    return cells


def diff_rows(field):
    return field[..., 1:, :] - field[..., :-1, :]


def diff_cols(field):
    return field[..., :, 1:] - field[..., :, :-1]


def back_rows(flux):
    return flux[..., :-1, :] - flux[..., 1:, :]


def back_cols(flux):
    return flux[..., :, :-1] - flux[..., :, 1:]


def centre_rows(field):
    return 0.5 * (field[..., 2:, :] - field[..., :-2, :])


def centre_cols(field):
    return 0.5 * (field[..., :, 2:] - field[..., :, :-2])


def operate(padded, eta_pad, fric):
    east = padded[0]
    north = padded[1]
    face_rows = 0.5 * (eta_pad[1:, :] + eta_pad[:-1, :])
    face_cols = 0.5 * (eta_pad[:, 1:] + eta_pad[:, :-1])

    def along_rows(field):
        return back_rows(face_rows * diff_rows(field))[:, 1:-1]

    def along_cols(field):
        return back_cols(face_cols * diff_cols(field))[1:-1, :]

    def mixed_rc(field):
        return centre_rows(eta_pad[:, 1:-1] * centre_cols(field))

    def mixed_cr(field):
        return centre_cols(eta_pad[1:-1, :] * centre_rows(field))

    out_east = (
        4.0 * along_rows(east)
        + along_cols(east)
        - 2.0 * mixed_rc(north)
        - mixed_cr(north)
        + fric * east[1:-1, 1:-1]
    )
    out_north = (
        along_rows(north)
        + 4.0 * along_cols(north)
        - 2.0 * mixed_cr(east)
        - mixed_rc(east)
        + fric * north[1:-1, 1:-1]
    )
    return jnp.stack([out_east, out_north])


def shards(
    adjoint_start,
    velocity,
    viscosity,
    friction,
    ice_mask,
    misfit,
    heading,
    row_dest,
    live_rows,
    pixel_lists,
):
    tile_rows, tile_cols = viscosity.shape
    count_gx = lax.axis_size("gx")
    count_gy = lax.axis_size("gy")
    tiles = count_gx * count_gy
    slots = pixel_lists.shape[1]
    width = misfit.shape[1]
    own_rows = misfit.shape[0]
    maskf = ice_mask.astype(jnp.float32)
    highest = lax.Precision.HIGHEST
    dest = row_dest[:, 0]
    onehot = (dest[:, None] == jnp.arange(tiles, dtype=jnp.int32)[None, :]).astype(jnp.bfloat16)
    row_ids = jnp.arange(own_rows, dtype=jnp.int32)
    earlier = (row_ids[:, None] > row_ids[None, :]).astype(jnp.bfloat16)
    before = jnp.dot(earlier, onehot, preferred_element_type=jnp.float32)
    slot = jnp.sum(before * onehot.astype(jnp.float32), axis=1).astype(jnp.int32)
    position = dest * slots + slot
    select = (position[:, None] == jnp.arange(tiles * slots, dtype=jnp.int32)[None, :]).astype(
        jnp.float32
    )
    live = (row_ids < live_rows[0]).astype(jnp.float32)
    values = (live[:, None] * misfit)[:, None, :] * jnp.stack(
        [jnp.cos(heading), jnp.sin(heading)], axis=1
    )[:, :, None]
    values = values.reshape(own_rows, 2 * width)
    outgoing = lax.dot_general(
        select,
        values,
        (((0,), (0,)), ((), ())),
        precision=highest,
        preferred_element_type=jnp.float32,
    )
    outgoing = outgoing.reshape(tiles, slots, 2, width)
    arrived = lax.all_to_all(outgoing, ("gx", "gy"), split_axis=0, concat_axis=0, tiled=True)
    pixels = tiles * slots * width
    block_len = width * math.gcd(tiles * slots, 32)
    turns = pixels // block_len
    pixel_rows = pixel_lists[:, :, 0, :].reshape(turns, block_len)
    pixel_cols = pixel_lists[:, :, 1, :].reshape(turns, block_len)
    value_east = arrived[:, :, 0, :].reshape(turns, block_len)
    value_north = arrived[:, :, 1, :].reshape(turns, block_len)
    row_iota = jnp.arange(tile_rows, dtype=jnp.int32)
    col_iota = jnp.arange(tile_cols, dtype=jnp.int32)

    def add_block(total, pieces):
        rows_here, cols_here, east_here, north_here = pieces
        row_hot = (rows_here[:, None] == row_iota[None, :]).astype(jnp.float32)
        col_hot = (cols_here[:, None] == col_iota[None, :]).astype(jnp.float32)
        weighted = jnp.concatenate(
            [row_hot * east_here[:, None], row_hot * north_here[:, None]], axis=1
        )
        term = lax.dot_general(
            weighted,
            col_hot,
            (((0,), (0,)), ((), ())),
            precision=highest,
            preferred_element_type=jnp.float32,
        )
        return (total + term, None)

    start_total = jnp.zeros((2 * tile_rows, tile_cols), jnp.float32)
    summed, _ = lax.scan(add_block, start_total, (pixel_rows, pixel_cols, value_east, value_north))
    load = summed.reshape(2, tile_rows, tile_cols) * maskf
    eta_pad = extended(viscosity, (("gx", 0), ("gy", 1)), 1)
    adjoint = adjoint_start
    for sweep in range(ITERS):
        masked = maskf * adjoint
        padded = extended(masked, (("gx", 1), ("gy", 2)), 1)
        image = maskf * operate(padded, eta_pad, friction) + (1.0 - maskf) * adjoint
        adjoint = adjoint + tau_step * (load - image)
    gradient = -maskf * friction * (velocity[0] * adjoint[0] + velocity[1] * adjoint[1])
    return (adjoint, gradient)


def solution(mesh):
    in_specs = (
        P(None, "gx", "gy"),
        P(None, "gx", "gy"),
        P("gx", "gy"),
        P("gx", "gy"),
        P("gx", "gy"),
        P(("gx", "gy"), None),
        P(("gx", "gy")),
        P(("gx", "gy"), None),
        P(("gx", "gy")),
        P(("gx", "gy"), None, None, None),
    )
    out_specs = (P(None, "gx", "gy"), P("gx", "gy"))
    return jax.shard_map(shards, mesh=mesh, in_specs=in_specs, out_specs=out_specs, check_vma=False)
```

profile of v0, /device:TPU:3, one launch (start us, length us, event | category | flops | bytes accessed | tf_op | source)
XLA Modules:
  0.0 481.9 jit_solution(11514567574666771848)
XLA Ops:
  2.6 3.8 collective-permute-start.4
  9.0 3.6 collective-permute-start
  21.2 10.7 %all-to-all-start = ((f32[128,8,2,128]{3,2,1,0:T(2,128)}), f32[128,8,2,128]{3,2,1,0:T(2,128)S(1)}, u32[]{:S(2)}, u32[]{:S(2)}) async-start(f32[128,8,2,128]{3,2,1,0:T(2,128)} %copy.17), calls=%async_computation | async-start | bytes 2097152 | tf_op jit(solution)/shard_map/all_to_all | solution.py:134
  32.1 3.2 collective-permute-start.6
  35.4 4.2 collective-permute-start.7
  39.5 3.3 slice_reduce_fusion.2
  42.9 8.0 %collective-permute-done.6 = f32[2,130,1]{2,1,0:T(8,128)S(1)} collective-permute-done((f32[2,130,1]{2,1,0:T(8,128)S(1)}, f32[2,130,1]{2,1,0:T(8,128)S(1)}, u32[]{:S(2)}, u32[]{:S(2)}) %collective-permute-start.6) | collective-permute-done | bytes 1072 | tf_op jit(solution)/shard_map/ppermute | solution.py:22
  54.0 5.7 %collective-permute-start.3 = (f32[130,1]{1,0:T(8,128)S(1)}, f32[130,1]{1,0:T(8,128)S(1)}, u32[]{:S(2)}, u32[]{:S(2)}) collective-permute-start(f32[130,1]{1,0:T(8,128)S(1)} %get-tuple-element.175), channel_id=1, source_target_pairs={{1,0},{2,1},{3,2},{4,3},{5,4},{6,5},{7,6},{8,7},{9,8},{10,9},{11,1... | collective-permute-start | bytes 1568 | tf_op jit(solution)/shard_map/ppermute | solution.py:24
  71.1 345.8 %while.11 = (s32[]{:T(128)}, f32[256,256]{1,0:T(8,128)S(1)}, s32[32,4096]{1,0:T(8,128)}, f32[32,4096]{1,0:T(8,128)}, f32[32,4096]{1,0:T(8,128)}, /*index=5*/s32[32,4096]{1,0:T(8,128)}, s32[]{:T(128)}, s32[]{:T(128)}) while((s32[]{:T(128)}, f32[256,256]{1,0:T(8,128)S(1)}, s32[32,4096]{1,0:T(8,128)}, f32[32,4096]{1,0:T(8,128)}, ...), condition=%wide.region_2.3_spmd.clone, body=%wide.region_1.2_spmd.clone.sunk | while | flops 3225026560 | bytes 9109607 | solution.py:162
  76.1 5.7 %fusion.204 = f32[256,256]{1,0:T(8,128)S(1)} fusion(s32[4096]{0:T(1024)S(1)} %bitcast.141, f32[4096,128]{1,0:T(8,128)} %get-tuple-element.248, f32[4096,128]{1,0:T(8,128)S(1)} %get-tuple-element.249, f32[256,256]{1,0:T(8,128)S(1)} %get-tuple-element.259, pred[]{:T(512)S(6)} %compare.3), kind=kOutput, calls=%fused_computation.11.clone.1 | convolution fusion | flops 3223453696 | bytes 4734977 | tf_op jit(solution)/shard_map/while/body/eval_jaxpr/dot_general | solution.py:152
  86.9 5.7 %fusion.204 = f32[256,256]{1,0:T(8,128)S(1)} fusion(s32[4096]{0:T(1024)S(1)} %bitcast.141, f32[4096,128]{1,0:T(8,128)} %get-tuple-element.248, f32[4096,128]{1,0:T(8,128)S(1)} %get-tuple-element.249, f32[256,256]{1,0:T(8,128)S(1)} %get-tuple-element.259, pred[]{:T(512)S(6)} %compare.3), kind=kOutput, calls=%fused_computation.11.clone.1 | convolution fusion | flops 3223453696 | bytes 4734977 | tf_op jit(solution)/shard_map/while/body/eval_jaxpr/dot_general | solution.py:152
  94.7 3.1 fusion.203
  97.7 5.7 %fusion.204 = f32[256,256]{1,0:T(8,128)S(1)} fusion(s32[4096]{0:T(1024)S(1)} %bitcast.141, f32[4096,128]{1,0:T(8,128)} %get-tuple-element.248, f32[4096,128]{1,0:T(8,128)S(1)} %get-tuple-element.249, f32[256,256]{1,0:T(8,128)S(1)} %get-tuple-element.259, pred[]{:T(512)S(6)} %compare.3), kind=kOutput, calls=%fused_computation.11.clone.1 | convolution fusion | flops 3223453696 | bytes 4734977 | tf_op jit(solution)/shard_map/while/body/eval_jaxpr/dot_general | solution.py:152
  108.5 5.7 %fusion.204 = f32[256,256]{1,0:T(8,128)S(1)} fusion(s32[4096]{0:T(1024)S(1)} %bitcast.141, f32[4096,128]{1,0:T(8,128)} %get-tuple-element.248, f32[4096,128]{1,0:T(8,128)S(1)} %get-tuple-element.249, f32[256,256]{1,0:T(8,128)S(1)} %get-tuple-element.259, pred[]{:T(512)S(6)} %compare.3), kind=kOutput, calls=%fused_computation.11.clone.1 | convolution fusion | flops 3223453696 | bytes 4734977 | tf_op jit(solution)/shard_map/while/body/eval_jaxpr/dot_general | solution.py:152
  116.3 3.1 fusion.203
  119.3 5.7 %fusion.204 = f32[256,256]{1,0:T(8,128)S(1)} fusion(s32[4096]{0:T(1024)S(1)} %bitcast.141, f32[4096,128]{1,0:T(8,128)} %get-tuple-element.248, f32[4096,128]{1,0:T(8,128)S(1)} %get-tuple-element.249, f32[256,256]{1,0:T(8,128)S(1)} %get-tuple-element.259, pred[]{:T(512)S(6)} %compare.3), kind=kOutput, calls=%fused_computation.11.clone.1 | convolution fusion | flops 3223453696 | bytes 4734977 | tf_op jit(solution)/shard_map/while/body/eval_jaxpr/dot_general | solution.py:152
  130.1 5.7 %fusion.204 = f32[256,256]{1,0:T(8,128)S(1)} fusion(s32[4096]{0:T(1024)S(1)} %bitcast.141, f32[4096,128]{1,0:T(8,128)} %get-tuple-element.248, f32[4096,128]{1,0:T(8,128)S(1)} %get-tuple-element.249, f32[256,256]{1,0:T(8,128)S(1)} %get-tuple-element.259, pred[]{:T(512)S(6)} %compare.3), kind=kOutput, calls=%fused_computation.11.clone.1 | convolution fusion | flops 3223453696 | bytes 4734977 | tf_op jit(solution)/shard_map/while/body/eval_jaxpr/dot_general | solution.py:152
  141.0 5.7 %fusion.204 = f32[256,256]{1,0:T(8,128)S(1)} fusion(s32[4096]{0:T(1024)S(1)} %bitcast.141, f32[4096,128]{1,0:T(8,128)} %get-tuple-element.248, f32[4096,128]{1,0:T(8,128)S(1)} %get-tuple-element.249, f32[256,256]{1,0:T(8,128)S(1)} %get-tuple-element.259, pred[]{:T(512)S(6)} %compare.3), kind=kOutput, calls=%fused_computation.11.clone.1 | convolution fusion | flops 3223453696 | bytes 4734977 | tf_op jit(solution)/shard_map/while/body/eval_jaxpr/dot_general | solution.py:152
  148.7 3.1 fusion.203
  151.8 5.7 %fusion.204 = f32[256,256]{1,0:T(8,128)S(1)} fusion(s32[4096]{0:T(1024)S(1)} %bitcast.141, f32[4096,128]{1,0:T(8,128)} %get-tuple-element.248, f32[4096,128]{1,0:T(8,128)S(1)} %get-tuple-element.249, f32[256,256]{1,0:T(8,128)S(1)} %get-tuple-element.259, pred[]{:T(512)S(6)} %compare.3), kind=kOutput, calls=%fused_computation.11.clone.1 | convolution fusion | flops 3223453696 | bytes 4734977 | tf_op jit(solution)/shard_map/while/body/eval_jaxpr/dot_general | solution.py:152
  162.6 5.7 %fusion.204 = f32[256,256]{1,0:T(8,128)S(1)} fusion(s32[4096]{0:T(1024)S(1)} %bitcast.141, f32[4096,128]{1,0:T(8,128)} %get-tuple-element.248, f32[4096,128]{1,0:T(8,128)S(1)} %get-tuple-element.249, f32[256,256]{1,0:T(8,128)S(1)} %get-tuple-element.259, pred[]{:T(512)S(6)} %compare.3), kind=kOutput, calls=%fused_computation.11.clone.1 | convolution fusion | flops 3223453696 | bytes 4734977 | tf_op jit(solution)/shard_map/while/body/eval_jaxpr/dot_general | solution.py:152
  170.3 3.1 fusion.203
  173.4 5.7 %fusion.204 = f32[256,256]{1,0:T(8,128)S(1)} fusion(s32[4096]{0:T(1024)S(1)} %bitcast.141, f32[4096,128]{1,0:T(8,128)} %get-tuple-element.248, f32[4096,128]{1,0:T(8,128)S(1)} %get-tuple-element.249, f32[256,256]{1,0:T(8,128)S(1)} %get-tuple-element.259, pred[]{:T(512)S(6)} %compare.3), kind=kOutput, calls=%fused_computation.11.clone.1 | convolution fusion | flops 3223453696 | bytes 4734977 | tf_op jit(solution)/shard_map/while/body/eval_jaxpr/dot_general | solution.py:152
  181.1 3.1 fusion.203
  184.2 5.7 %fusion.204 = f32[256,256]{1,0:T(8,128)S(1)} fusion(s32[4096]{0:T(1024)S(1)} %bitcast.141, f32[4096,128]{1,0:T(8,128)} %get-tuple-element.248, f32[4096,128]{1,0:T(8,128)S(1)} %get-tuple-element.249, f32[256,256]{1,0:T(8,128)S(1)} %get-tuple-element.259, pred[]{:T(512)S(6)} %compare.3), kind=kOutput, calls=%fused_computation.11.clone.1 | convolution fusion | flops 3223453696 | bytes 4734977 | tf_op jit(solution)/shard_map/while/body/eval_jaxpr/dot_general | solution.py:152
  191.9 3.1 fusion.203
  195.0 5.7 %fusion.204 = f32[256,256]{1,0:T(8,128)S(1)} fusion(s32[4096]{0:T(1024)S(1)} %bitcast.141, f32[4096,128]{1,0:T(8,128)} %get-tuple-element.248, f32[4096,128]{1,0:T(8,128)S(1)} %get-tuple-element.249, f32[256,256]{1,0:T(8,128)S(1)} %get-tuple-element.259, pred[]{:T(512)S(6)} %compare.3), kind=kOutput, calls=%fused_computation.11.clone.1 | convolution fusion | flops 3223453696 | bytes 4734977 | tf_op jit(solution)/shard_map/while/body/eval_jaxpr/dot_general | solution.py:152
  202.7 3.1 fusion.203
  205.8 5.7 %fusion.204 = f32[256,256]{1,0:T(8,128)S(1)} fusion(s32[4096]{0:T(1024)S(1)} %bitcast.141, f32[4096,128]{1,0:T(8,128)} %get-tuple-element.248, f32[4096,128]{1,0:T(8,128)S(1)} %get-tuple-element.249, f32[256,256]{1,0:T(8,128)S(1)} %get-tuple-element.259, pred[]{:T(512)S(6)} %compare.3), kind=kOutput, calls=%fused_computation.11.clone.1 | convolution fusion | flops 3223453696 | bytes 4734977 | tf_op jit(solution)/shard_map/while/body/eval_jaxpr/dot_general | solution.py:152
  213.5 3.1 fusion.203
  216.6 5.7 %fusion.204 = f32[256,256]{1,0:T(8,128)S(1)} fusion(s32[4096]{0:T(1024)S(1)} %bitcast.141, f32[4096,128]{1,0:T(8,128)} %get-tuple-element.248, f32[4096,128]{1,0:T(8,128)S(1)} %get-tuple-element.249, f32[256,256]{1,0:T(8,128)S(1)} %get-tuple-element.259, pred[]{:T(512)S(6)} %compare.3), kind=kOutput, calls=%fused_computation.11.clone.1 | convolution fusion | flops 3223453696 | bytes 4734977 | tf_op jit(solution)/shard_map/while/body/eval_jaxpr/dot_general | solution.py:152
  224.3 3.1 fusion.203
  227.4 5.7 %fusion.204 = f32[256,256]{1,0:T(8,128)S(1)} fusion(s32[4096]{0:T(1024)S(1)} %bitcast.141, f32[4096,128]{1,0:T(8,128)} %get-tuple-element.248, f32[4096,128]{1,0:T(8,128)S(1)} %get-tuple-element.249, f32[256,256]{1,0:T(8,128)S(1)} %get-tuple-element.259, pred[]{:T(512)S(6)} %compare.3), kind=kOutput, calls=%fused_computation.11.clone.1 | convolution fusion | flops 3223453696 | bytes 4734977 | tf_op jit(solution)/shard_map/while/body/eval_jaxpr/dot_general | solution.py:152
  235.1 3.1 fusion.203
  238.2 5.7 %fusion.204 = f32[256,256]{1,0:T(8,128)S(1)} fusion(s32[4096]{0:T(1024)S(1)} %bitcast.141, f32[4096,128]{1,0:T(8,128)} %get-tuple-element.248, f32[4096,128]{1,0:T(8,128)S(1)} %get-tuple-element.249, f32[256,256]{1,0:T(8,128)S(1)} %get-tuple-element.259, pred[]{:T(512)S(6)} %compare.3), kind=kOutput, calls=%fused_computation.11.clone.1 | convolution fusion | flops 3223453696 | bytes 4734977 | tf_op jit(solution)/shard_map/while/body/eval_jaxpr/dot_general | solution.py:152
  249.0 5.7 %fusion.204 = f32[256,256]{1,0:T(8,128)S(1)} fusion(s32[4096]{0:T(1024)S(1)} %bitcast.141, f32[4096,128]{1,0:T(8,128)} %get-tuple-element.248, f32[4096,128]{1,0:T(8,128)S(1)} %get-tuple-element.249, f32[256,256]{1,0:T(8,128)S(1)} %get-tuple-element.259, pred[]{:T(512)S(6)} %compare.3), kind=kOutput, calls=%fused_computation.11.clone.1 | convolution fusion | flops 3223453696 | bytes 4734977 | tf_op jit(solution)/shard_map/while/body/eval_jaxpr/dot_general | solution.py:152
  256.8 3.1 fusion.203
  259.8 5.7 %fusion.204 = f32[256,256]{1,0:T(8,128)S(1)} fusion(s32[4096]{0:T(1024)S(1)} %bitcast.141, f32[4096,128]{1,0:T(8,128)} %get-tuple-element.248, f32[4096,128]{1,0:T(8,128)S(1)} %get-tuple-element.249, f32[256,256]{1,0:T(8,128)S(1)} %get-tuple-element.259, pred[]{:T(512)S(6)} %compare.3), kind=kOutput, calls=%fused_computation.11.clone.1 | convolution fusion | flops 3223453696 | bytes 4734977 | tf_op jit(solution)/shard_map/while/body/eval_jaxpr/dot_general | solution.py:152
  270.6 5.7 %fusion.204 = f32[256,256]{1,0:T(8,128)S(1)} fusion(s32[4096]{0:T(1024)S(1)} %bitcast.141, f32[4096,128]{1,0:T(8,128)} %get-tuple-element.248, f32[4096,128]{1,0:T(8,128)S(1)} %get-tuple-element.249, f32[256,256]{1,0:T(8,128)S(1)} %get-tuple-element.259, pred[]{:T(512)S(6)} %compare.3), kind=kOutput, calls=%fused_computation.11.clone.1 | convolution fusion | flops 3223453696 | bytes 4734977 | tf_op jit(solution)/shard_map/while/body/eval_jaxpr/dot_general | solution.py:152
  278.4 3.1 fusion.203
  281.4 5.7 %fusion.204 = f32[256,256]{1,0:T(8,128)S(1)} fusion(s32[4096]{0:T(1024)S(1)} %bitcast.141, f32[4096,128]{1,0:T(8,128)} %get-tuple-element.248, f32[4096,128]{1,0:T(8,128)S(1)} %get-tuple-element.249, f32[256,256]{1,0:T(8,128)S(1)} %get-tuple-element.259, pred[]{:T(512)S(6)} %compare.3), kind=kOutput, calls=%fused_computation.11.clone.1 | convolution fusion | flops 3223453696 | bytes 4734977 | tf_op jit(solution)/shard_map/while/body/eval_jaxpr/dot_general | solution.py:152
  289.2 3.1 fusion.203
  292.2 5.7 %fusion.204 = f32[256,256]{1,0:T(8,128)S(1)} fusion(s32[4096]{0:T(1024)S(1)} %bitcast.141, f32[4096,128]{1,0:T(8,128)} %get-tuple-element.248, f32[4096,128]{1,0:T(8,128)S(1)} %get-tuple-element.249, f32[256,256]{1,0:T(8,128)S(1)} %get-tuple-element.259, pred[]{:T(512)S(6)} %compare.3), kind=kOutput, calls=%fused_computation.11.clone.1 | convolution fusion | flops 3223453696 | bytes 4734977 | tf_op jit(solution)/shard_map/while/body/eval_jaxpr/dot_general | solution.py:152
  300.0 3.1 fusion.203
  303.0 5.7 %fusion.204 = f32[256,256]{1,0:T(8,128)S(1)} fusion(s32[4096]{0:T(1024)S(1)} %bitcast.141, f32[4096,128]{1,0:T(8,128)} %get-tuple-element.248, f32[4096,128]{1,0:T(8,128)S(1)} %get-tuple-element.249, f32[256,256]{1,0:T(8,128)S(1)} %get-tuple-element.259, pred[]{:T(512)S(6)} %compare.3), kind=kOutput, calls=%fused_computation.11.clone.1 | convolution fusion | flops 3223453696 | bytes 4734977 | tf_op jit(solution)/shard_map/while/body/eval_jaxpr/dot_general | solution.py:152
  310.8 3.1 fusion.203
  313.8 5.7 %fusion.204 = f32[256,256]{1,0:T(8,128)S(1)} fusion(s32[4096]{0:T(1024)S(1)} %bitcast.141, f32[4096,128]{1,0:T(8,128)} %get-tuple-element.248, f32[4096,128]{1,0:T(8,128)S(1)} %get-tuple-element.249, f32[256,256]{1,0:T(8,128)S(1)} %get-tuple-element.259, pred[]{:T(512)S(6)} %compare.3), kind=kOutput, calls=%fused_computation.11.clone.1 | convolution fusion | flops 3223453696 | bytes 4734977 | tf_op jit(solution)/shard_map/while/body/eval_jaxpr/dot_general | solution.py:152
  321.6 3.1 fusion.203
  324.6 5.7 %fusion.204 = f32[256,256]{1,0:T(8,128)S(1)} fusion(s32[4096]{0:T(1024)S(1)} %bitcast.141, f32[4096,128]{1,0:T(8,128)} %get-tuple-element.248, f32[4096,128]{1,0:T(8,128)S(1)} %get-tuple-element.249, f32[256,256]{1,0:T(8,128)S(1)} %get-tuple-element.259, pred[]{:T(512)S(6)} %compare.3), kind=kOutput, calls=%fused_computation.11.clone.1 | convolution fusion | flops 3223453696 | bytes 4734977 | tf_op jit(solution)/shard_map/while/body/eval_jaxpr/dot_general | solution.py:152
  335.4 5.7 %fusion.204 = f32[256,256]{1,0:T(8,128)S(1)} fusion(s32[4096]{0:T(1024)S(1)} %bitcast.141, f32[4096,128]{1,0:T(8,128)} %get-tuple-element.248, f32[4096,128]{1,0:T(8,128)S(1)} %get-tuple-element.249, f32[256,256]{1,0:T(8,128)S(1)} %get-tuple-element.259, pred[]{:T(512)S(6)} %compare.3), kind=kOutput, calls=%fused_computation.11.clone.1 | convolution fusion | flops 3223453696 | bytes 4734977 | tf_op jit(solution)/shard_map/while/body/eval_jaxpr/dot_general | solution.py:152
  346.3 5.7 %fusion.204 = f32[256,256]{1,0:T(8,128)S(1)} fusion(s32[4096]{0:T(1024)S(1)} %bitcast.141, f32[4096,128]{1,0:T(8,128)} %get-tuple-element.248, f32[4096,128]{1,0:T(8,128)S(1)} %get-tuple-element.249, f32[256,256]{1,0:T(8,128)S(1)} %get-tuple-element.259, pred[]{:T(512)S(6)} %compare.3), kind=kOutput, calls=%fused_computation.11.clone.1 | convolution fusion | flops 3223453696 | bytes 4734977 | tf_op jit(solution)/shard_map/while/body/eval_jaxpr/dot_general | solution.py:152
  357.1 5.7 %fusion.204 = f32[256,256]{1,0:T(8,128)S(1)} fusion(s32[4096]{0:T(1024)S(1)} %bitcast.141, f32[4096,128]{1,0:T(8,128)} %get-tuple-element.248, f32[4096,128]{1,0:T(8,128)S(1)} %get-tuple-element.249, f32[256,256]{1,0:T(8,128)S(1)} %get-tuple-element.259, pred[]{:T(512)S(6)} %compare.3), kind=kOutput, calls=%fused_computation.11.clone.1 | convolution fusion | flops 3223453696 | bytes 4734977 | tf_op jit(solution)/shard_map/while/body/eval_jaxpr/dot_general | solution.py:152
  367.9 5.7 %fusion.204 = f32[256,256]{1,0:T(8,128)S(1)} fusion(s32[4096]{0:T(1024)S(1)} %bitcast.141, f32[4096,128]{1,0:T(8,128)} %get-tuple-element.248, f32[4096,128]{1,0:T(8,128)S(1)} %get-tuple-element.249, f32[256,256]{1,0:T(8,128)S(1)} %get-tuple-element.259, pred[]{:T(512)S(6)} %compare.3), kind=kOutput, calls=%fused_computation.11.clone.1 | convolution fusion | flops 3223453696 | bytes 4734977 | tf_op jit(solution)/shard_map/while/body/eval_jaxpr/dot_general | solution.py:152
  378.7 5.7 %fusion.204 = f32[256,256]{1,0:T(8,128)S(1)} fusion(s32[4096]{0:T(1024)S(1)} %bitcast.141, f32[4096,128]{1,0:T(8,128)} %get-tuple-element.248, f32[4096,128]{1,0:T(8,128)S(1)} %get-tuple-element.249, f32[256,256]{1,0:T(8,128)S(1)} %get-tuple-element.259, pred[]{:T(512)S(6)} %compare.3), kind=kOutput, calls=%fused_computation.11.clone.1 | convolution fusion | flops 3223453696 | bytes 4734977 | tf_op jit(solution)/shard_map/while/body/eval_jaxpr/dot_general | solution.py:152
  389.5 5.7 %fusion.204 = f32[256,256]{1,0:T(8,128)S(1)} fusion(s32[4096]{0:T(1024)S(1)} %bitcast.141, f32[4096,128]{1,0:T(8,128)} %get-tuple-element.248, f32[4096,128]{1,0:T(8,128)S(1)} %get-tuple-element.249, f32[256,256]{1,0:T(8,128)S(1)} %get-tuple-element.259, pred[]{:T(512)S(6)} %compare.3), kind=kOutput, calls=%fused_computation.11.clone.1 | convolution fusion | flops 3223453696 | bytes 4734977 | tf_op jit(solution)/shard_map/while/body/eval_jaxpr/dot_general | solution.py:152
  400.3 5.7 %fusion.204 = f32[256,256]{1,0:T(8,128)S(1)} fusion(s32[4096]{0:T(1024)S(1)} %bitcast.141, f32[4096,128]{1,0:T(8,128)} %get-tuple-element.248, f32[4096,128]{1,0:T(8,128)S(1)} %get-tuple-element.249, f32[256,256]{1,0:T(8,128)S(1)} %get-tuple-element.259, pred[]{:T(512)S(6)} %compare.3), kind=kOutput, calls=%fused_computation.11.clone.1 | convolution fusion | flops 3223453696 | bytes 4734977 | tf_op jit(solution)/shard_map/while/body/eval_jaxpr/dot_general | solution.py:152
  411.1 5.7 %fusion.204 = f32[256,256]{1,0:T(8,128)S(1)} fusion(s32[4096]{0:T(1024)S(1)} %bitcast.141, f32[4096,128]{1,0:T(8,128)} %get-tuple-element.248, f32[4096,128]{1,0:T(8,128)S(1)} %get-tuple-element.249, f32[256,256]{1,0:T(8,128)S(1)} %get-tuple-element.259, pred[]{:T(512)S(6)} %compare.3), kind=kOutput, calls=%fused_computation.11.clone.1 | convolution fusion | flops 3223453696 | bytes 4734977 | tf_op jit(solution)/shard_map/while/body/eval_jaxpr/dot_general | solution.py:152
  418.0 4.1 collective-permute-start.8
  429.0 5.5 %collective-permute-start.11 = (f32[2,130,1]{2,1,0:T(8,128)S(1)}, f32[2,130,1]{2,1,0:T(8,128)S(1)}, u32[]{:S(2)}, u32[]{:S(2)}) collective-permute-start(f32[2,130,1]{2,1,0:T(8,128)S(1)} %get-tuple-element.125), channel_id=1, source_target_pairs={{1,0},{2,1},{3,2},{4,3},{5,4},{6,5},{7,6},{8,7},{9,8},{10,9},{11,1... | collective-permute-start | bytes 3128 | tf_op jit(solution)/shard_map/ppermute | solution.py:24
  438.9 3.9 collective-permute-start.12
  450.6 5.7 %collective-permute-start.15 = (f32[2,130,1]{2,1,0:T(8,128)S(1)}, f32[2,130,1]{2,1,0:T(8,128)S(1)}, u32[]{:S(2)}, u32[]{:S(2)}) collective-permute-start(f32[2,130,1]{2,1,0:T(8,128)S(1)} %get-tuple-element.123), channel_id=1, source_target_pairs={{1,0},{2,1},{3,2},{4,3},{5,4},{6,5},{7,6},{8,7},{9,8},{10,9},{11,1... | collective-permute-start | bytes 3128 | tf_op jit(solution)/shard_map/ppermute | solution.py:24
  459.6 4.2 collective-permute-start.16
  468.8 3.2 collective-permute-start.18
  472.1 4.9 %collective-permute-start.19 = (f32[2,130,1]{2,1,0:T(8,128)S(1)}, f32[2,130,1]{2,1,0:T(8,128)S(1)}, u32[]{:S(2)}, u32[]{:S(2)}) collective-permute-start(f32[2,130,1]{2,1,0:T(8,128)S(1)} %get-tuple-element.121), channel_id=1, source_target_pairs={{1,0},{2,1},{3,2},{4,3},{5,4},{6,5},{7,6},{8,7},{9,8},{10,9},{11,1... | collective-permute-start | bytes 3128 | tf_op jit(solution)/shard_map/ppermute | solution.py:24
  (220 shorter events, 172.9 us)
Async XLA Ops:
  0.6 17.6 %copy-start.13 = (s32[512,1]{0,1:T(1,128)S(1)}, s32[512,1]{0,1:T(1,128)}, u32[]{:S(2)}) copy-start(s32[512,1]{0,1:T(1,128)} %param.19) | copy-start | bytes 6148
  2.6 29.4 %collective-permute-start.4 = (f32[2,1,256]{2,1,0:T(1,128)S(1)}, f32[2,1,256]{2,1,0:T(1,128)S(1)}, u32[]{:S(2)}, u32[]{:S(2)}) collective-permute-start(f32[2,1,256]{2,1,0:T(1,128)S(1)} %get-tuple-element.134), channel_id=1, source_target_pairs={{0,16},{16,32},{32,48},{48,64},{64,80},{80,96},{96,112},{1,17},{17... | collective-permute-start | bytes 6152 | tf_op jit(solution)/shard_map/ppermute | solution.py:22
  6.3 25.6 %collective-permute-start.5 = (f32[2,1,256]{2,1,0:T(1,128)S(1)}, f32[2,1,256]{2,1,0:T(1,128)S(1)}, u32[]{:S(2)}, u32[]{:S(2)}) collective-permute-start(f32[2,1,256]{2,1,0:T(1,128)S(1)} %get-tuple-element.135), channel_id=1, source_target_pairs={{16,0},{32,16},{48,32},{64,48},{80,64},{96,80},{112,96},{17,1},{33... | collective-permute-start | bytes 6152 | tf_op jit(solution)/shard_map/ppermute | solution.py:24
  9.0 42.2 %collective-permute-start = (f32[1,256]{1,0:T(1,128)S(1)}, f32[1,256]{1,0:T(1,128)S(1)}, u32[]{:S(2)}, u32[]{:S(2)}) collective-permute-start(f32[1,256]{1,0:T(1,128)S(1)} %get-tuple-element.193), channel_id=1, source_target_pairs={{0,16},{16,32},{32,48},{48,64},{64,80},{80,96},{96,112},{1,17},{17... | collective-permute-start | bytes 3080 | tf_op jit(solution)/shard_map/ppermute | solution.py:22
  12.6 38.5 %collective-permute-start.1 = (f32[1,256]{1,0:T(1,128)S(1)}, f32[1,256]{1,0:T(1,128)S(1)}, u32[]{:S(2)}, u32[]{:S(2)}) collective-permute-start(f32[1,256]{1,0:T(1,128)S(1)} %get-tuple-element.194), channel_id=1, source_target_pairs={{16,0},{32,16},{48,32},{64,48},{80,64},{96,80},{112,96},{17,1},{33... | collective-permute-start | bytes 3080 | tf_op jit(solution)/shard_map/ppermute | solution.py:24
  21.2 18.3 %copy-start.8 = (s32[128,8,2,128]{3,2,1,0:T(2,128)S(1)}, s32[128,8,2,128]{3,2,1,0:T(2,128)}, u32[]{:S(2)}) copy-start(s32[128,8,2,128]{3,2,1,0:T(2,128)} %param.21) | copy-start | bytes 3145732
  21.2 45.2 %all-to-all-start = ((f32[128,8,2,128]{3,2,1,0:T(2,128)}), f32[128,8,2,128]{3,2,1,0:T(2,128)S(1)}, u32[]{:S(2)}, u32[]{:S(2)}) async-start(f32[128,8,2,128]{3,2,1,0:T(2,128)} %copy.17), calls=%async_computation | async-start | bytes 2097152 | tf_op jit(solution)/shard_map/all_to_all | solution.py:134
  32.0 19.2 %copy-start = (f32[128,256]{1,0:T(8,128)S(1)}, f32[128,256]{1,0:T(8,128)}, u32[]{:S(2)}) copy-start(f32[128,256]{1,0:T(8,128)} %param.14) | copy-start | bytes 393220
  32.1 18.8 %collective-permute-start.6 = (f32[2,130,1]{2,1,0:T(8,128)S(1)}, f32[2,130,1]{2,1,0:T(8,128)S(1)}, u32[]{:S(2)}, u32[]{:S(2)}) collective-permute-start(f32[2,130,1]{2,1,0:T(8,128)S(1)} %get-tuple-element.126), channel_id=1, source_target_pairs={{0,1},{1,2},{2,3},{3,4},{4,5},{5,6},{6,7},{7,8},{8,9},{9,10},{10,1... | collective-permute-start | bytes 3128 | tf_op jit(solution)/shard_map/ppermute | solution.py:22
  35.4 15.5 %collective-permute-start.7 = (f32[2,130,1]{2,1,0:T(8,128)S(1)}, f32[2,130,1]{2,1,0:T(8,128)S(1)}, u32[]{:S(2)}, u32[]{:S(2)}) collective-permute-start(f32[2,130,1]{2,1,0:T(8,128)S(1)} %get-tuple-element.127), channel_id=1, source_target_pairs={{1,0},{2,1},{3,2},{4,3},{5,4},{6,5},{7,6},{8,7},{9,8},{10,9},{11,1... | collective-permute-start | bytes 3128 | tf_op jit(solution)/shard_map/ppermute | solution.py:24
  42.9 16.8 %copy-start.3 = (s32[128,256]{1,0:T(8,128)S(1)}, s32[128,256]{1,0:T(8,128)}, u32[]{:S(2)}) copy-start(s32[128,256]{1,0:T(8,128)} %param.16) | copy-start | bytes 393220
  52.0 10.5 %collective-permute-start.2 = (f32[130,1]{1,0:T(8,128)S(1)}, f32[130,1]{1,0:T(8,128)S(1)}, u32[]{:S(2)}, u32[]{:S(2)}) collective-permute-start(f32[130,1]{1,0:T(8,128)S(1)} %get-tuple-element.174), channel_id=1, source_target_pairs={{0,1},{1,2},{2,3},{3,4},{4,5},{5,6},{6,7},{7,8},{8,9},{9,10},{10,1... | collective-permute-start | bytes 1568 | tf_op jit(solution)/shard_map/ppermute | solution.py:22
  54.0 8.5 %collective-permute-start.3 = (f32[130,1]{1,0:T(8,128)S(1)}, f32[130,1]{1,0:T(8,128)S(1)}, u32[]{:S(2)}, u32[]{:S(2)}) collective-permute-start(f32[130,1]{1,0:T(8,128)S(1)} %get-tuple-element.175), channel_id=1, source_target_pairs={{1,0},{2,1},{3,2},{4,3},{5,4},{6,5},{7,6},{8,7},{9,8},{10,9},{11,1... | collective-permute-start | bytes 1568 | tf_op jit(solution)/shard_map/ppermute | solution.py:24
  62.5 0.6 copy-start.10
  63.3 0.9 copy-start.11
  64.4 0.9 copy-start.1
  64.4 1.0 copy-start.7
  418.0 6.0 %collective-permute-start.8 = (f32[2,1,256]{2,1,0:T(1,128)S(1)}, f32[2,1,256]{2,1,0:T(1,128)S(1)}, u32[]{:S(2)}, u32[]{:S(2)}) collective-permute-start(f32[2,1,256]{2,1,0:T(1,128)S(1)} %get-tuple-element.132), channel_id=1, source_target_pairs={{0,16},{16,32},{32,48},{48,64},{64,80},{80,96},{96,112},{1,17},{17... | collective-permute-start | bytes 6152 | tf_op jit(solution)/shard_map/ppermute | solution.py:22
  422.1 4.9 %collective-permute-start.9 = (f32[2,1,256]{2,1,0:T(1,128)S(1)}, f32[2,1,256]{2,1,0:T(1,128)S(1)}, u32[]{:S(2)}, u32[]{:S(2)}) collective-permute-start(f32[2,1,256]{2,1,0:T(1,128)S(1)} %get-tuple-element.133), channel_id=1, source_target_pairs={{16,0},{32,16},{48,32},{64,48},{80,64},{96,80},{112,96},{17,1},{33... | collective-permute-start | bytes 6152 | tf_op jit(solution)/shard_map/ppermute | solution.py:24
  427.1 8.0 %collective-permute-start.10 = (f32[2,130,1]{2,1,0:T(8,128)S(1)}, f32[2,130,1]{2,1,0:T(8,128)S(1)}, u32[]{:S(2)}, u32[]{:S(2)}) collective-permute-start(f32[2,130,1]{2,1,0:T(8,128)S(1)} %get-tuple-element.124), channel_id=1, source_target_pairs={{0,1},{1,2},{2,3},{3,4},{4,5},{5,6},{6,7},{7,8},{8,9},{9,10},{10,1... | collective-permute-start | bytes 3128 | tf_op jit(solution)/shard_map/ppermute | solution.py:22
  429.0 7.8 %collective-permute-start.11 = (f32[2,130,1]{2,1,0:T(8,128)S(1)}, f32[2,130,1]{2,1,0:T(8,128)S(1)}, u32[]{:S(2)}, u32[]{:S(2)}) collective-permute-start(f32[2,130,1]{2,1,0:T(8,128)S(1)} %get-tuple-element.125), channel_id=1, source_target_pairs={{1,0},{2,1},{3,2},{4,3},{5,4},{6,5},{7,6},{8,7},{9,8},{10,9},{11,1... | collective-permute-start | bytes 3128 | tf_op jit(solution)/shard_map/ppermute | solution.py:24
  437.7 1.0 copy-start.2
  437.7 1.0 copy-start.5
  437.7 1.0 copy-start.6
  438.9 5.9 %collective-permute-start.12 = (f32[2,1,256]{2,1,0:T(1,128)S(1)}, f32[2,1,256]{2,1,0:T(1,128)S(1)}, u32[]{:S(2)}, u32[]{:S(2)}) collective-permute-start(f32[2,1,256]{2,1,0:T(1,128)S(1)} %get-tuple-element.130), channel_id=1, source_target_pairs={{0,16},{16,32},{32,48},{48,64},{64,80},{80,96},{96,112},{1,17},{17... | collective-permute-start | bytes 6152 | tf_op jit(solution)/shard_map/ppermute | solution.py:22
  442.8 4.9 %collective-permute-start.13 = (f32[2,1,256]{2,1,0:T(1,128)S(1)}, f32[2,1,256]{2,1,0:T(1,128)S(1)}, u32[]{:S(2)}, u32[]{:S(2)}) collective-permute-start(f32[2,1,256]{2,1,0:T(1,128)S(1)} %get-tuple-element.131), channel_id=1, source_target_pairs={{16,0},{32,16},{48,32},{64,48},{80,64},{96,80},{112,96},{17,1},{33... | collective-permute-start | bytes 6152 | tf_op jit(solution)/shard_map/ppermute | solution.py:24
  447.9 8.7 %collective-permute-start.14 = (f32[2,130,1]{2,1,0:T(8,128)S(1)}, f32[2,130,1]{2,1,0:T(8,128)S(1)}, u32[]{:S(2)}, u32[]{:S(2)}) collective-permute-start(f32[2,130,1]{2,1,0:T(8,128)S(1)} %get-tuple-element.122), channel_id=1, source_target_pairs={{0,1},{1,2},{2,3},{3,4},{4,5},{5,6},{6,7},{7,8},{8,9},{9,10},{10,1... | collective-permute-start | bytes 3128 | tf_op jit(solution)/shard_map/ppermute | solution.py:22
  450.6 7.5 %collective-permute-start.15 = (f32[2,130,1]{2,1,0:T(8,128)S(1)}, f32[2,130,1]{2,1,0:T(8,128)S(1)}, u32[]{:S(2)}, u32[]{:S(2)}) collective-permute-start(f32[2,130,1]{2,1,0:T(8,128)S(1)} %get-tuple-element.123), channel_id=1, source_target_pairs={{1,0},{2,1},{3,2},{4,3},{5,4},{6,5},{7,6},{8,7},{9,8},{10,9},{11,1... | collective-permute-start | bytes 3128 | tf_op jit(solution)/shard_map/ppermute | solution.py:24
  459.6 6.1 %collective-permute-start.16 = (f32[2,1,256]{2,1,0:T(1,128)S(1)}, f32[2,1,256]{2,1,0:T(1,128)S(1)}, u32[]{:S(2)}, u32[]{:S(2)}) collective-permute-start(f32[2,1,256]{2,1,0:T(1,128)S(1)} %get-tuple-element.128), channel_id=1, source_target_pairs={{0,16},{16,32},{32,48},{48,64},{64,80},{80,96},{96,112},{1,17},{17... | collective-permute-start | bytes 6152 | tf_op jit(solution)/shard_map/ppermute | solution.py:22
  463.8 4.9 %collective-permute-start.17 = (f32[2,1,256]{2,1,0:T(1,128)S(1)}, f32[2,1,256]{2,1,0:T(1,128)S(1)}, u32[]{:S(2)}, u32[]{:S(2)}) collective-permute-start(f32[2,1,256]{2,1,0:T(1,128)S(1)} %get-tuple-element.129), channel_id=1, source_target_pairs={{16,0},{32,16},{48,32},{64,48},{80,64},{96,80},{112,96},{17,1},{33... | collective-permute-start | bytes 6152 | tf_op jit(solution)/shard_map/ppermute | solution.py:24
  468.8 8.7 %collective-permute-start.18 = (f32[2,130,1]{2,1,0:T(8,128)S(1)}, f32[2,130,1]{2,1,0:T(8,128)S(1)}, u32[]{:S(2)}, u32[]{:S(2)}) collective-permute-start(f32[2,130,1]{2,1,0:T(8,128)S(1)} %get-tuple-element.120), channel_id=1, source_target_pairs={{0,1},{1,2},{2,3},{3,4},{4,5},{5,6},{6,7},{7,8},{8,9},{9,10},{10,1... | collective-permute-start | bytes 3128 | tf_op jit(solution)/shard_map/ppermute | solution.py:22
  472.1 7.0 %collective-permute-start.19 = (f32[2,130,1]{2,1,0:T(8,128)S(1)}, f32[2,130,1]{2,1,0:T(8,128)S(1)}, u32[]{:S(2)}, u32[]{:S(2)}) collective-permute-start(f32[2,130,1]{2,1,0:T(8,128)S(1)} %get-tuple-element.121), channel_id=1, source_target_pairs={{1,0},{2,1},{3,2},{4,3},{5,4},{6,5},{7,6},{8,7},{9,8},{10,9},{11,1... | collective-permute-start | bytes 3128 | tf_op jit(solution)/shard_map/ppermute | solution.py:24
  480.1 0.9 copy-start.4
  480.1 1.0 copy-start.12
  481.2 0.7 copy-start.9
where the time goes:
time: 486 us; the launch traced here: 482 us
  matrix products  185 us (38%)
  other arithmetic  109 us (22%)
  local copies, waits for them, and re-layouts  82.4 us (17%)
  starting transfers between devices  78.8 us (16%)
  waiting for transfers between devices  23.3 us (5%)
    dot_general x32, matrix products, add_block(): lax.dot_general(weighted, col_hot, (((0,), (0,)), ((), ())), precision=hi...  183 us
    mul x32, other arithmetic, add_block(): row_hot * east_here[:, None]  97.9 us
    dynamic_slice x64, local copies, waits for them, and re-layouts, shards(): lax.scan(add_block, start_total, (pixel_rows, pixel_cols, value_east, val...  63.9 us
    ppermute x10, starting transfers between devices, extended(): lax.ppermute(head, axis, [((i + 1) % count, i) for i in range(ends)])  35.5 us
    ppermute x10, starting transfers between devices, extended(): lax.ppermute(tail, axis, [(i, (i + 1) % count) for i in range(ends)])  32.6 us
    ppermute x10, waiting for transfers between devices, extended(): lax.ppermute(head, axis, [((i + 1) % count, i) for i in range(ends)])  13.8 us
    all_to_all x1, starting transfers between devices, shards(): lax.all_to_all(outgoing, ('gx', 'gy'), split_axis=0, concat_axis=0, tiled...  10.7 us
  transfers between devices with their start and end apart: 21, of which 10 were waited for; matrix products, arithmetic and copies ran while one was open for 3% of the time, Pallas kernels for 0%

commit v1 on v0

v1 whole, which is shorter than its diff:
```python
import functools

import jax
import jax.numpy as jnp
from jax import lax
from jax.experimental import pallas as pl
from jax.experimental.pallas import tpu as pltpu
from jax.sharding import PartitionSpec as P

ITERS = 4
TAU = 0.04
MESH = pl.DeviceIdType.MESH
F32 = jnp.float32
BF16 = jnp.bfloat16
NT = (((1,), (1,)), ((), ()))
NN = (((1,), (0,)), ((), ()))


def mm(a, b, dims=NN):
    return lax.dot_general(a, b, dims, preferred_element_type=F32)


def halves(x):
    high = x.astype(BF16)
    return high, (x - high.astype(F32)).astype(BF16)


def hot(ids, count, sub):
    base = lax.broadcasted_iota(jnp.int32, (count, ids.shape[1]), 0).astype(F32).astype(BF16)
    return [base[i : i + sub] == ids for i in range(0, count, sub)]


def route(live_ref, dest_ref, heading_ref, misfit_ref, out_ref):
    tiles = out_ref.shape[0]
    own = misfit_ref.shape[0]
    dest = dest_ref[...]
    row_id = lax.broadcasted_iota(jnp.int32, (1, own), 1)
    live = row_id < live_ref[0]
    one = lax.broadcasted_iota(jnp.int32, (tiles, own), 0) == dest
    onehot = jnp.where(one, 1.0, 0.0)
    earlier = jnp.where(
        lax.broadcasted_iota(jnp.int32, (own, own), 0) < lax.broadcasted_iota(jnp.int32, (own, own), 1),
        1.0,
        0.0,
    ).astype(BF16)
    before = mm(onehot.astype(BF16), earlier)
    slot = jnp.sum(before * onehot, axis=0, keepdims=True).astype(jnp.int32)
    position = jnp.where(live, dest * 8 + slot, -1)
    angle = heading_ref[...]
    v_high, v_low = halves(misfit_ref[...])
    step = 256
    for first in range(0, tiles * 8, step):
        here = lax.broadcasted_iota(jnp.int32, (step, own), 0) + first == position
        for comp, factor in enumerate((jnp.cos(angle), jnp.sin(angle))):
            f_high, f_low = halves(factor)
            s_high = jnp.where(here, f_high.astype(F32), 0.0).astype(BF16)
            s_low = jnp.where(here, f_low.astype(F32), 0.0).astype(BF16)
            part = mm(s_high, v_high) + (mm(s_high, v_low) + mm(s_low, v_high))
            out_ref[first // 8 : (first + step) // 8, 8 * comp : 8 * comp + 8, :] = part.reshape(step // 8, 8, 128)


def scatter_group(rows8, cols8, values, acc_ref):
    left, right = [], []
    sub = 16
    zero = jnp.zeros((sub, 128), BF16)
    unit = jnp.ones((sub, 128), BF16)
    for rows, cols, pair in zip(rows8, cols8, values):
        for k in range(8):
            r = jnp.broadcast_to(rows[k : k + 1].astype(F32), (sub, 128)).astype(BF16)
            c = jnp.broadcast_to(cols[k : k + 1].astype(F32), (sub, 128)).astype(BF16)
            pieces = []
            for v in pair:
                pieces += halves(jnp.broadcast_to(v[k : k + 1], (sub, 128)))
            at_row = hot(r, 128, sub)
            left.append(jnp.concatenate([jnp.where(m, p, zero) for p in pieces for m in at_row], axis=0))
            right.append(jnp.concatenate([jnp.where(m, unit, zero) for m in hot(c, 256, sub)], axis=0))
    acc_ref[...] += mm(jnp.concatenate(left, axis=1), jnp.concatenate(right, axis=1), NT)


def scatter(lists_ref, values_ref, load_ref, acc):
    tiles = values_ref.shape[0]
    group = 8
    acc[...] = jnp.zeros_like(acc)

    def step(t, carry):
        sources = [t * group + q for q in range(group)]
        scatter_group(
            [lists_ref[s, :, 0, :] for s in sources],
            [lists_ref[s, :, 1, :] for s in sources],
            [(values_ref[s, 0:8, :], values_ref[s, 8:16, :]) for s in sources],
            acc,
        )
        return carry

    lax.fori_loop(0, tiles // group, step, 0)
    load_ref[0] = acc[0:128] + acc[128:256]
    load_ref[1] = acc[256:384] + acc[384:512]


def neighbours(gx, gy, n_gx, n_gy):
    found = []
    for dx in (-1, 0, 1):
        for dy in (-1, 0, 1):
            if dx or dy:
                found.append((dx, dy, lax.rem(gx + dx + n_gx, n_gx), lax.rem(gy + dy + n_gy, n_gy)))
    return found


def pack_rows(field):
    first = lax.broadcasted_iota(jnp.int32, (8, 256), 0) < 4
    return jnp.where(first, field[0:8], field[120:128])


def pack_cols(field):
    first = lax.broadcasted_iota(jnp.int32, (128, 128), 1) < 64
    return jnp.where(first, field[:, 0:128], field[:, 128:256])


def up(f):
    return pltpu.roll(f, f.shape[0] - 1, 0)


def down(f):
    return pltpu.roll(f, 1, 0)


def right(f):
    return pltpu.roll(f, f.shape[1] - 1, 1)


def left(f):
    return pltpu.roll(f, 1, 1)


def apply(e, n, eta, cx, cy, fric):
    e_up, e_right = up(e), right(e)
    n_up, n_right = up(n), right(n)
    ge = 0.5 * eta * (e_up - down(e))
    he = 0.5 * eta * (e_right - left(e))
    gn = 0.5 * eta * (n_up - down(n))
    hn = 0.5 * eta * (n_right - left(n))
    pe, qe = 4.0 * cx * (e_up - e), cy * (e_right - e)
    pn, qn = cx * (n_up - n), 4.0 * cy * (n_right - n)
    gn, he = 0.5 * gn, 0.5 * he
    out_e = down(pe + hn) - pe - up(hn) + left(qe + gn) - qe - right(gn) + fric * e
    out_n = down(pn + he) - pn - up(he) + left(qn + ge) - qn - right(ge) + fric * n
    return out_e, out_n


def stencil(
    n_gx,
    n_gy,
    load_ref,
    start_ref,
    visc_ref,
    fric_ref,
    mask_ref,
    vel_ref,
    adj_ref,
    grad_ref,
    ext,
    send_rows,
    send_cols,
    got_rows,
    got_cols,
    got_corners,
    send_sem,
    recv_sem,
):
    gx, gy = lax.axis_index("gx"), lax.axis_index("gy")
    around = neighbours(gx, gy, n_gx, n_gy)
    barrier = pltpu.get_barrier_semaphore()
    for _, _, x, y in around:
        pl.semaphore_signal(barrier, inc=1, device_id=(x, y), device_id_type=MESH)
    fields = [load_ref[0], load_ref[1], start_ref[0], start_ref[1], visc_ref[...], fric_ref[...], mask_ref[...].astype(F32)]
    for i, f in enumerate(fields):
        ext[i, 0:128, 0:256] = f
        send_rows[i] = pack_rows(f)
        send_cols[i] = pack_cols(f)
        send_corner = jnp.where(
            lax.broadcasted_iota(jnp.int32, (8, 128), 0) < 4, send_cols[i, 0:8], send_cols[i, 120:128]
        )
        send_cols[i + len(fields), 0:8] = send_corner
    pl.semaphore_wait(barrier, 8)
    copies = []
    for slot, (dx, dy, x, y) in enumerate(around):
        if dy == 0:
            src, dst = send_rows, got_rows.at[(dx + 1) // 2]
        elif dx == 0:
            src, dst = send_cols.at[0:7], got_cols.at[(dy + 1) // 2]
        else:
            src, dst = send_cols.at[7:14, 0:8], got_corners.at[(dx + 1) + (dy + 1) // 2]
        copy = pltpu.make_async_remote_copy(
            src_ref=src,
            dst_ref=dst,
            send_sem=send_sem.at[slot],
            recv_sem=recv_sem.at[slot],
            device_id=(x, y),
            device_id_type=MESH,
        )
        copy.start()
        copies.append(copy)
    for copy in copies:
        copy.wait()
    has = lambda ok, value: jnp.where(ok, value, 0.0)
    top, bottom, west, east = gx > 0, gx < n_gx - 1, gy > 0, gy < n_gy - 1
    both = jnp.logical_and
    for i in range(7):
        sub = lax.broadcasted_iota(jnp.int32, (8, 256), 0) < 4
        ext[i, 128:136, 0:256] = jnp.where(sub, has(bottom, got_rows[0, i]), has(top, got_rows[1, i]))
        lane = lax.broadcasted_iota(jnp.int32, (128, 128), 1)
        value = jnp.where(lane < 64, has(east, got_cols[0, i]), has(west, got_cols[1, i]))
        ext[i, 0:128, 256:384] = jnp.where((lane < 4) | (lane >= 124), value, 0.0)
        lane = lax.broadcasted_iota(jnp.int32, (8, 128), 1)
        sub = lax.broadcasted_iota(jnp.int32, (8, 128), 0) < 4
        below = jnp.where(lane < 64, has(both(bottom, east), got_corners[0, i]), has(both(bottom, west), got_corners[1, i]))
        above = jnp.where(lane < 64, has(both(top, east), got_corners[2, i]), has(both(top, west), got_corners[3, i]))
        value = jnp.where(sub, below, above)
        ext[i, 128:136, 256:384] = jnp.where((lane < 4) | (lane >= 124), value, 0.0)
    eta, fric, mask = ext[4], ext[5], ext[6]
    cx, cy = 0.5 * (eta + up(eta)), 0.5 * (eta + right(eta))
    ext[7], ext[8] = cx, cy
    weight = TAU * mask
    ext[9] = weight
    ext[0] = weight * ext[0]
    ext[1] = weight * ext[1]
    ext[2] = mask * ext[2]
    ext[3] = mask * ext[3]

    def sweep(_, carry):
        out_e, out_n = apply(ext[2], ext[3], ext[4], ext[7], ext[8], ext[5])
        ext[2] = ext[2] + (ext[0] - ext[9] * out_e)
        ext[3] = ext[3] + (ext[1] - ext[9] * out_n)
        return carry

    lax.fori_loop(0, ITERS, sweep, 0)
    on_ice = mask_ref[...] > 0
    keep = (1.0 - TAU) ** ITERS
    w_e, w_n = ext[2, 0:128, 0:256], ext[3, 0:128, 0:256]
    adj_ref[0] = jnp.where(on_ice, w_e, keep * start_ref[0])
    adj_ref[1] = jnp.where(on_ice, w_n, keep * start_ref[1])
    grad_ref[...] = -(fric_ref[...] * (vel_ref[0] * w_e + vel_ref[1] * w_n))


VMEM = pl.BlockSpec(memory_space=pltpu.VMEM)
SMEM = pl.BlockSpec(memory_space=pltpu.SMEM)


def shards(n_gx, n_gy, start, velocity, viscosity, friction, ice_mask, misfit, heading, row_dest, live_rows, lists):
    tiles = n_gx * n_gy
    own = misfit.shape[0]
    outgoing = pl.pallas_call(
        route,
        out_shape=jax.ShapeDtypeStruct((tiles, 16, 128), F32),
        in_specs=[SMEM, VMEM, VMEM, VMEM],
        out_specs=VMEM,
        compiler_params=pltpu.CompilerParams(vmem_limit_bytes=32 << 20),
        name="route",
    )(live_rows, row_dest.reshape(1, own), heading.reshape(1, own), misfit)
    arrived = lax.all_to_all(outgoing, ("gx", "gy"), split_axis=0, concat_axis=0, tiled=True)
    load = pl.pallas_call(
        scatter,
        out_shape=jax.ShapeDtypeStruct((2, 128, 256), F32),
        in_specs=[VMEM] * 2,
        out_specs=VMEM,
        scratch_shapes=[pltpu.VMEM((512, 256), F32)],
        compiler_params=pltpu.CompilerParams(vmem_limit_bytes=40 << 20),
        name="scatter",
    )(lists, arrived)
    return pl.pallas_call(
        functools.partial(stencil, n_gx, n_gy),
        out_shape=(jax.ShapeDtypeStruct((2, 128, 256), F32), jax.ShapeDtypeStruct((128, 256), F32)),
        in_specs=[VMEM] * 6,
        out_specs=(VMEM, VMEM),
        scratch_shapes=[
            pltpu.VMEM((10, 136, 384), F32),
            pltpu.VMEM((7, 8, 256), F32),
            pltpu.VMEM((14, 128, 128), F32),
            pltpu.VMEM((2, 7, 8, 256), F32),
            pltpu.VMEM((2, 7, 128, 128), F32),
            pltpu.VMEM((4, 7, 8, 128), F32),
            pltpu.SemaphoreType.DMA((8,)),
            pltpu.SemaphoreType.DMA((8,)),
        ],
        compiler_params=pltpu.CompilerParams(collective_id=0, has_side_effects=True, vmem_limit_bytes=40 << 20),
        name="stencil",
    )(load, start, viscosity, friction, ice_mask, velocity)


def solution(mesh):
    in_specs = (
        P(None, "gx", "gy"),
        P(None, "gx", "gy"),
        P("gx", "gy"),
        P("gx", "gy"),
        P("gx", "gy"),
        P(("gx", "gy"), None),
        P(("gx", "gy")),
        P(("gx", "gy"), None),
        P(("gx", "gy")),
        P(("gx", "gy"), None, None, None),
    )
    return jax.shard_map(
        functools.partial(shards, mesh.shape["gx"], mesh.shape["gy"]),
        mesh=mesh,
        in_specs=in_specs,
        out_specs=(P(None, "gx", "gy"), P("gx", "gy")),
        check_vma=False,
    )
```

time: 486 us -> 96.7 us (0.20)
  the two profiles are of different devices: /device:TPU:3 before, /device:TPU:0 now
where the time goes in v1:
time: 96.7 us; the launch traced here: 96.5 us
  Pallas kernels  62.1 us (64%)
  blocking collectives  30 us (31%)
  local copies, waits for them, and re-layouts  3.01 us (3%)
  between operations  1.4 us (1%)
    pallas_call x1, Pallas kernels, shards(): pl.pallas_call(scatter, out_shape=jax.ShapeDtypeStruct((2, 128, 256), F32...  37.9 us
    all_to_all x1, blocking collectives, shards(): lax.all_to_all(outgoing, ('gx', 'gy'), split_axis=0, concat_axis=0, tiled...  30 us
    pallas_call x1, Pallas kernels, shards(): pl.pallas_call(functools.partial(stencil, n_gx, n_gy), out_shape=(jax.Sha...  22.1 us
    unnamed x20, local copies, waits for them, and re-layouts  3.01 us
    pallas_call x1, Pallas kernels, shards(): pl.pallas_call(route, out_shape=jax.ShapeDtypeStruct((tiles, 16, 128), F3...  2.05 us

profile of v1, /device:TPU:0, one launch (start us, length us, event | category | flops | bytes accessed | tf_op | source)
XLA Modules:
  0.0 96.5 jit_solution(9487329280638847664)
XLA Ops:
  0.6 0.0 copy-start.8
  1.3 0.0 copy-start.7
  1.3 0.0 copy-done.8
  1.3 0.7 copy-done.7
  2.0 0.0 copy-start.1
  2.0 0.9 copy-done.1
  2.9 2.1 %route.1 = f32[128,16,128]{2,1,0:T(8,128)S(1)} custom-call(s32[1]{0:T(128)S(6)} %copy.14.live_ref, s32[1,512]{1,0:T(1,128)S(1)} %bitcast.2, f32[1,512]{1,0:T(1,128)S(1)} %bitcast.3, f32[512,128]{1,0:T(8,128)S(1)} %copy-done.1), custom_call_target="tpu_custom_call" | custom-call | tf_op jit(solution)/shard_map/route/pallas_call | solution.py:252
  5.0 0.0 copy-start
  5.0 30.0 %all_to_all.5.values_ref = f32[128,16,128]{2,1,0:T(8,128)S(1)} all-to-all(f32[128,16,128]{2,1,0:T(8,128)S(1)} %route.1), channel_id=1, replica_groups=mesh['gx'=8,'gy'=16] {'gx','gy'}, dimensions={0} | all-to-all | bytes 2097152 | tf_op jit(solution)/shard_map/all_to_all | solution.py:260
  35.0 0.0 copy-done
  35.0 0.0 copy-start.2
  35.0 0.0 copy-start.3
  35.0 0.0 copy-start.4
  35.0 0.0 copy-start.5
  35.0 0.0 copy-start.6
  35.0 37.9 %scatter.1.load_ref = f32[2,128,256]{2,1,0:T(8,128)S(1)} custom-call(s32[128,8,2,128]{3,2,1,0:T(2,128)S(1)} %copy-done, f32[128,16,128]{2,1,0:T(8,128)S(1)} %all_to_all.5.values_ref), custom_call_target="tpu_custom_call" | custom-call | tf_op jit(solution)/shard_map/scatter/pallas_call | solution.py:261
  72.9 0.0 copy-done.2
  72.9 0.0 copy-done.3
  72.9 0.0 copy-done.4
  72.9 0.0 copy-done.5
  73.0 0.0 copy-done.6
  73.0 22.1 %stencil.1 = (f32[2,128,256]{2,1,0:T(8,128)S(1)}, f32[128,256]{1,0:T(8,128)S(1)}) custom-call(f32[2,128,256]{2,1,0:T(8,128)S(1)} %scatter.1.load_ref, f32[2,128,256]{2,1,0:T(8,128)S(1)} %copy-done.2, f32[128,256]{1,0:T(8,128)S(1)} %copy-done.4, f32[128,256]{1,0:T(8,128)S(1)} %copy-done.5, s32[128,256]{1,0:T(8,128)S(1)} %copy-done.6, f32[2,128,256]{2,1,0:T(8,128)S(1)} %copy-done.3), custom_call_target="tpu_custom_call" | custom-call | tf_op jit(solution)/shard_map/stencil/pallas_call | solution.py:270
  95.1 0.7 copy.15
  95.8 0.7 copy.16
Async XLA Ops:
  0.6 0.7 copy-start.8
  1.3 0.7 copy-start.7
  2.0 0.9 copy-start.1
  5.0 30.0 %copy-start = (s32[128,8,2,128]{3,2,1,0:T(2,128)S(1)}, s32[128,8,2,128]{3,2,1,0:T(2,128)}, u32[]{:S(2)}) copy-start(s32[128,8,2,128]{3,2,1,0:T(2,128)} %lists_ref.1) | copy-start | bytes 3145732
  35.0 37.9 %copy-start.2 = (f32[2,128,256]{2,1,0:T(8,128)S(1)}, f32[2,128,256]{2,1,0:T(8,128)}, u32[]{:S(2)}) copy-start(f32[2,128,256]{2,1,0:T(8,128)} %start_ref.1) | copy-start | bytes 786436
  35.0 37.9 %copy-start.3 = (f32[2,128,256]{2,1,0:T(8,128)S(1)}, f32[2,128,256]{2,1,0:T(8,128)}, u32[]{:S(2)}) copy-start(f32[2,128,256]{2,1,0:T(8,128)} %vel_ref.1) | copy-start | bytes 786436
  35.0 37.9 %copy-start.4 = (f32[128,256]{1,0:T(8,128)S(1)}, f32[128,256]{1,0:T(8,128)}, u32[]{:S(2)}) copy-start(f32[128,256]{1,0:T(8,128)} %visc_ref.1) | copy-start | bytes 393220
  35.0 37.9 %copy-start.5 = (f32[128,256]{1,0:T(8,128)S(1)}, f32[128,256]{1,0:T(8,128)}, u32[]{:S(2)}) copy-start(f32[128,256]{1,0:T(8,128)} %fric_ref.1) | copy-start | bytes 393220
  35.0 37.9 %copy-start.6 = (s32[128,256]{1,0:T(8,128)S(1)}, s32[128,256]{1,0:T(8,128)}, u32[]{:S(2)}) copy-start(s32[128,256]{1,0:T(8,128)} %mask_ref.1) | copy-start | bytes 393220

commit v2 on v1

v2 whole, which is shorter than its diff:
```python
import functools

import jax
import jax.numpy as jnp
from jax import lax
from jax.experimental import pallas as pl
from jax.experimental.pallas import tpu as pltpu
from jax.sharding import PartitionSpec as P

ITERS = 4
TAU = 0.04
MESH = pl.DeviceIdType.MESH
F32 = jnp.float32
BF16 = jnp.bfloat16
NT = (((1,), (1,)), ((), ()))
NN = (((1,), (0,)), ((), ()))


def mm(a, b, dims=NN):
    return lax.dot_general(a, b, dims, preferred_element_type=F32)


def halves(x):
    high = x.astype(BF16)
    return high, (x - high.astype(F32)).astype(BF16)


def hot(ids, count, sub):
    base = lax.broadcasted_iota(jnp.int32, (count, ids.shape[1]), 0).astype(F32).astype(BF16)
    return [base[i : i + sub] == ids for i in range(0, count, sub)]


def route(live_ref, dest_ref, heading_ref, misfit_ref, out_ref):
    tiles = out_ref.shape[0]
    own = misfit_ref.shape[0]
    dest = dest_ref[...]
    row_id = lax.broadcasted_iota(jnp.int32, (1, own), 1)
    live = row_id < live_ref[0]
    one = lax.broadcasted_iota(jnp.int32, (tiles, own), 0) == dest
    onehot = jnp.where(one, 1.0, 0.0)
    earlier = jnp.where(
        lax.broadcasted_iota(jnp.int32, (own, own), 0) < lax.broadcasted_iota(jnp.int32, (own, own), 1),
        1.0,
        0.0,
    ).astype(BF16)
    before = mm(onehot.astype(BF16), earlier)
    slot = jnp.sum(before * onehot, axis=0, keepdims=True).astype(jnp.int32)
    position = jnp.where(live, dest * 8 + slot, -1)
    angle = heading_ref[...]
    v_high, v_low = halves(misfit_ref[...])
    step = 256
    for first in range(0, tiles * 8, step):
        here = lax.broadcasted_iota(jnp.int32, (step, own), 0) + first == position
        for comp, factor in enumerate((jnp.cos(angle), jnp.sin(angle))):
            f_high, f_low = halves(factor)
            s_high = jnp.where(here, f_high.astype(F32), 0.0).astype(BF16)
            s_low = jnp.where(here, f_low.astype(F32), 0.0).astype(BF16)
            part = mm(s_high, v_high) + (mm(s_high, v_low) + mm(s_low, v_high))
            out_ref[first // 8 : (first + step) // 8, 8 * comp : 8 * comp + 8, :] = part.reshape(step // 8, 8, 128)


def scatter_group(rows8, cols8, values, acc_ref):
    left, right = [], []
    sub = 16
    zero = jnp.zeros((sub, 128), BF16)
    unit = jnp.ones((sub, 128), BF16)
    for rows, cols, pair in zip(rows8, cols8, values):
        for k in range(8):
            r = jnp.broadcast_to(rows[k : k + 1].astype(F32), (sub, 128)).astype(BF16)
            c = jnp.broadcast_to(cols[k : k + 1].astype(F32), (sub, 128)).astype(BF16)
            pieces = []
            for v in pair:
                pieces += halves(jnp.broadcast_to(v[k : k + 1], (sub, 128)))
            at_row = hot(r, 128, sub)
            left.append(jnp.concatenate([jnp.where(m, p, zero) for p in pieces for m in at_row], axis=0))
            right.append(jnp.concatenate([jnp.where(m, unit, zero) for m in hot(c, 256, sub)], axis=0))
    acc_ref[...] += mm(jnp.concatenate(left, axis=1), jnp.concatenate(right, axis=1), NT)


def neighbours(gx, gy, n_gx, n_gy):
    found = []
    for dx in (-1, 0, 1):
        for dy in (-1, 0, 1):
            if dx or dy:
                found.append((dx, dy, lax.rem(gx + dx + n_gx, n_gx), lax.rem(gy + dy + n_gy, n_gy)))
    return found


def pack_rows(field):
    first = lax.broadcasted_iota(jnp.int32, (8, 256), 0) < 4
    return jnp.where(first, field[0:8], field[120:128])


def pack_cols(field):
    first = lax.broadcasted_iota(jnp.int32, (128, 128), 1) < 64
    return jnp.where(first, field[:, 0:128], field[:, 128:256])


def up(f):
    return pltpu.roll(f, f.shape[0] - 1, 0)


def down(f):
    return pltpu.roll(f, 1, 0)


def right(f):
    return pltpu.roll(f, f.shape[1] - 1, 1)


def left(f):
    return pltpu.roll(f, 1, 1)


def apply(e, n, eta, cx, cy, fric):
    e_up, e_right = up(e), right(e)
    n_up, n_right = up(n), right(n)
    ge = 0.5 * eta * (e_up - down(e))
    he = 0.5 * eta * (e_right - left(e))
    gn = 0.5 * eta * (n_up - down(n))
    hn = 0.5 * eta * (n_right - left(n))
    pe, qe = 4.0 * cx * (e_up - e), cy * (e_right - e)
    pn, qn = cx * (n_up - n), 4.0 * cy * (n_right - n)
    gn, he = 0.5 * gn, 0.5 * he
    out_e = down(pe + hn) - pe - up(hn) + left(qe + gn) - qe - right(gn) + fric * e
    out_n = down(pn + he) - pn - up(he) + left(qn + ge) - qn - right(ge) + fric * n
    return out_e, out_n


def fill_edges(ext, fields, flags, rows, cols, corners):
    top, bottom, west, east = flags
    has = lambda ok, value: jnp.where(ok, value, 0.0)
    both = jnp.logical_and
    for i, field in enumerate(fields):
        sub = lax.broadcasted_iota(jnp.int32, (8, 256), 0) < 4
        ext[field, 128:136, 0:256] = jnp.where(sub, has(bottom, rows[0, i]), has(top, rows[1, i]))
        lane = lax.broadcasted_iota(jnp.int32, (128, 128), 1)
        value = jnp.where(lane < 64, has(east, cols[0, i]), has(west, cols[1, i]))
        ext[field, 0:128, 256:384] = jnp.where((lane < 4) | (lane >= 124), value, 0.0)
        lane = lax.broadcasted_iota(jnp.int32, (8, 128), 1)
        sub = lax.broadcasted_iota(jnp.int32, (8, 128), 0) < 4
        below = jnp.where(lane < 64, has(both(bottom, east), corners[0, i]), has(both(bottom, west), corners[1, i]))
        above = jnp.where(lane < 64, has(both(top, east), corners[2, i]), has(both(top, west), corners[3, i]))
        value = jnp.where(sub, below, above)
        ext[field, 128:136, 256:384] = jnp.where((lane < 4) | (lane >= 124), value, 0.0)


def edge_copies(around, packed, got, sems):
    rows, cols, corner = packed
    got_rows, got_cols, got_corners = got
    copies = []
    for slot, (dx, dy, x, y) in enumerate(around):
        if dy == 0:
            src, dst = rows, got_rows.at[(dx + 1) // 2]
        elif dx == 0:
            src, dst = cols, got_cols.at[(dy + 1) // 2]
        else:
            src, dst = corner, got_corners.at[(dx + 1) + (dy + 1) // 2]
        copies.append(
            pltpu.make_async_remote_copy(
                src_ref=src,
                dst_ref=dst,
                send_sem=sems.at[0, slot],
                recv_sem=sems.at[1, slot],
                device_id=(x, y),
                device_id_type=MESH,
            )
        )
    return copies


def pack_edge(i, field, packed):
    rows, cols, corner = packed
    rows[i] = pack_rows(field)
    cols[i] = pack_cols(field)
    first = lax.broadcasted_iota(jnp.int32, (8, 128), 0) < 4
    corner[i] = jnp.where(first, cols[i, 0:8], cols[i, 120:128])


def body(
    n_gx,
    n_gy,
    live_ref,
    dest_hbm,
    heading_hbm,
    misfit_hbm,
    start_hbm,
    visc_hbm,
    fric_hbm,
    mask_hbm,
    vel_hbm,
    lists_hbm,
    adj_ref,
    grad_ref,
    dest_ref,
    heading_ref,
    misfit_ref,
    start_ref,
    visc_ref,
    fric_ref,
    mask_ref,
    vel_ref,
    lists,
    outgoing,
    arrived,
    acc,
    ext,
    fixed_rows,
    fixed_cols,
    fixed_corner,
    fixed_got_rows,
    fixed_got_cols,
    fixed_got_corners,
    load_rows,
    load_cols,
    load_corner,
    load_got_rows,
    load_got_cols,
    load_got_corners,
    in_sems,
    send_sem,
    recv_sem,
    fixed_sems,
    load_sems,
    all_sem,
):
    gx, gy = lax.axis_index("gx"), lax.axis_index("gy")
    me = gx * n_gy + gy
    around = neighbours(gx, gy, n_gx, n_gy)
    loads = [
        pltpu.make_async_copy(src, dst, in_sems.at[i])
        for i, (src, dst) in enumerate(
            [
                (dest_hbm, dest_ref),
                (heading_hbm, heading_ref),
                (misfit_hbm, misfit_ref),
                (start_hbm, start_ref),
                (visc_hbm, visc_ref),
                (fric_hbm, fric_ref),
                (mask_hbm, mask_ref),
                (lists_hbm, lists),
                (vel_hbm, vel_ref),
            ]
        )
    ]
    for copy in loads:
        copy.start()

    barrier = pltpu.get_barrier_semaphore()
    for a in range(1, n_gx):
        pl.semaphore_signal(barrier, inc=1, device_id=(lax.rem(gx + a, n_gx), gy), device_id_type=MESH)
    for b in range(1, n_gy):
        pl.semaphore_signal(barrier, inc=1, device_id=(gx, lax.rem(gy + b, n_gy)), device_id_type=MESH)

    for copy in loads[0:3]:
        copy.wait()
    route(live_ref, dest_ref, heading_ref, misfit_ref, outgoing)
    acc[...] = jnp.zeros_like(acc)
    fixed_packed = (fixed_rows, fixed_cols, fixed_corner)
    for copy in loads[3:7]:
        copy.wait()
    fields = [start_ref[0], start_ref[1], visc_ref[...], fric_ref[...], mask_ref[...].astype(F32)]
    for i, f in enumerate(fields):
        ext[2 + i, 0:128, 0:256] = f
        pack_edge(i, f, fixed_packed)

    pl.semaphore_wait(barrier, n_gx + n_gy - 2)
    for b in range(1, n_gy):
        pl.semaphore_signal(all_sem, inc=1, device_id=(gx, lax.rem(gy + b, n_gy)), device_id_type=MESH)
    pl.semaphore_wait(all_sem, n_gy - 1)

    fixed_got = (fixed_got_rows, fixed_got_cols, fixed_got_corners)
    fixed_copies = edge_copies(around, fixed_packed, fixed_got, fixed_sems)
    for copy in fixed_copies:
        copy.start()

    def send_group(g, first=0):
        y = lax.rem(gy + g, n_gy)
        for a in range(first, n_gx):
            x = lax.rem(gx + a, n_gx)
            pltpu.make_async_remote_copy(
                src_ref=outgoing.at[x * n_gy + y],
                dst_ref=arrived.at[gy, gx],
                send_sem=send_sem,
                recv_sem=recv_sem.at[g],
                device_id=(x, y),
                device_id_type=MESH,
            ).start()

    pltpu.make_async_copy(outgoing.at[me], arrived.at[gy, gx], recv_sem.at[0]).start()
    send_group(0, 1)
    send_group(1)

    for copy in fixed_copies:
        copy.wait_recv()
    flags = (gx > 0, gx < n_gx - 1, gy > 0, gy < n_gy - 1)
    fill_edges(ext, range(2, 7), flags, *fixed_got)
    eta, fric, mask = ext[4], ext[5], ext[6]
    ext[7], ext[8] = 0.5 * (eta + up(eta)), 0.5 * (eta + right(eta))
    ext[9] = TAU * mask
    ext[2] = mask * ext[2]
    ext[3] = mask * ext[3]
    out_e, out_n = apply(ext[2], ext[3], ext[4], ext[7], ext[8], ext[5])
    ext[2] = ext[2] - ext[9] * out_e
    ext[3] = ext[3] - ext[9] * out_n
    for copy in loads[7:9]:
        copy.wait()

    def take_group(g):
        y = lax.rem(gy + n_gy - g, n_gy)
        pltpu.make_async_copy(outgoing.at[0:n_gx], arrived.at[y], recv_sem.at[g]).wait()
        sources = [x * n_gy + y for x in range(n_gx)]
        scatter_group(
            [lists[s, :, 0, :] for s in sources],
            [lists[s, :, 1, :] for s in sources],
            [(arrived[y, x, 0:8, :], arrived[y, x, 8:16, :]) for x in range(n_gx)],
            acc,
        )

    def send_and_take(g, carry):
        send_group(g + 2)
        take_group(g)
        return carry

    def take(g, carry):
        take_group(g)
        return carry

    lax.fori_loop(0, n_gy - 2, send_and_take, 0)
    lax.fori_loop(n_gy - 2, n_gy, take, 0)

    load_packed = (load_rows, load_cols, load_corner)
    for i in range(2):
        f = acc[256 * i : 256 * i + 128] + acc[256 * i + 128 : 256 * i + 256]
        ext[i, 0:128, 0:256] = f
        pack_edge(i, f, load_packed)
    load_got = (load_got_rows, load_got_cols, load_got_corners)
    load_copies = edge_copies(around, load_packed, load_got, load_sems)
    for copy in load_copies:
        copy.start()
    for copy in load_copies:
        copy.wait_recv()
    fill_edges(ext, range(2), flags, *load_got)
    ext[0] = ext[9] * ext[0]
    ext[1] = ext[9] * ext[1]
    ext[2] = ext[2] + ext[0]
    ext[3] = ext[3] + ext[1]

    def sweep(_, carry):
        out_e, out_n = apply(ext[2], ext[3], ext[4], ext[7], ext[8], ext[5])
        ext[2] = ext[2] + (ext[0] - ext[9] * out_e)
        ext[3] = ext[3] + (ext[1] - ext[9] * out_n)
        return carry

    lax.fori_loop(0, ITERS - 1, sweep, 0)
    on_ice = mask_ref[...] > 0
    keep = (1.0 - TAU) ** ITERS
    w_e, w_n = ext[2, 0:128, 0:256], ext[3, 0:128, 0:256]
    adj_ref[0] = jnp.where(on_ice, w_e, keep * start_ref[0])
    adj_ref[1] = jnp.where(on_ice, w_n, keep * start_ref[1])
    grad_ref[...] = -(fric_ref[...] * (vel_ref[0] * w_e + vel_ref[1] * w_n))

    for copy in fixed_copies + load_copies:
        copy.wait_send()
    sent = n_gx * n_gy - 1
    pltpu.make_async_remote_copy(
        src_ref=outgoing.at[0:sent],
        dst_ref=outgoing.at[0:sent],
        send_sem=send_sem,
        recv_sem=recv_sem.at[0],
        device_id=(gx, gy),
        device_id_type=MESH,
    ).wait_send()


VMEM = pl.BlockSpec(memory_space=pltpu.VMEM)
SMEM = pl.BlockSpec(memory_space=pltpu.SMEM)
HBM = pl.BlockSpec(memory_space=pltpu.HBM)


def edge_scratch(fields):
    return [
        pltpu.VMEM((fields, 8, 256), F32),
        pltpu.VMEM((fields, 128, 128), F32),
        pltpu.VMEM((fields, 8, 128), F32),
        pltpu.VMEM((2, fields, 8, 256), F32),
        pltpu.VMEM((2, fields, 128, 128), F32),
        pltpu.VMEM((4, fields, 8, 128), F32),
    ]


def shards(n_gx, n_gy, start, velocity, viscosity, friction, ice_mask, misfit, heading, row_dest, live_rows, lists):
    tiles = n_gx * n_gy
    own = misfit.shape[0]
    return pl.pallas_call(
        functools.partial(body, n_gx, n_gy),
        out_shape=(jax.ShapeDtypeStruct((2, 128, 256), F32), jax.ShapeDtypeStruct((128, 256), F32)),
        in_specs=[SMEM] + [HBM] * 9,
        out_specs=(VMEM, VMEM),
        scratch_shapes=[
            pltpu.VMEM((1, own), jnp.int32),
            pltpu.VMEM((1, own), F32),
            pltpu.VMEM(misfit.shape, F32),
            pltpu.VMEM(start.shape, F32),
            pltpu.VMEM(viscosity.shape, F32),
            pltpu.VMEM(friction.shape, F32),
            pltpu.VMEM(ice_mask.shape, jnp.int32),
            pltpu.VMEM(velocity.shape, F32),
            pltpu.VMEM(lists.shape, jnp.int32),
            pltpu.VMEM((tiles, 16, 128), F32),
            pltpu.VMEM((n_gy, n_gx, 16, 128), F32),
            pltpu.VMEM((512, 256), F32),
            pltpu.VMEM((10, 136, 384), F32),
            *edge_scratch(5),
            *edge_scratch(2),
            pltpu.SemaphoreType.DMA((9,)),
            pltpu.SemaphoreType.DMA,
            pltpu.SemaphoreType.DMA((n_gy,)),
            pltpu.SemaphoreType.DMA((2, 8)),
            pltpu.SemaphoreType.DMA((2, 8)),
            pltpu.SemaphoreType.REGULAR,
        ],
        compiler_params=pltpu.CompilerParams(collective_id=0, has_side_effects=True, vmem_limit_bytes=60 << 20),
        name="shelf",
    )(
        live_rows,
        row_dest.reshape(1, own),
        heading.reshape(1, own),
        misfit,
        start,
        viscosity,
        friction,
        ice_mask,
        velocity,
        lists,
    )


def solution(mesh):
    in_specs = (
        P(None, "gx", "gy"),
        P(None, "gx", "gy"),
        P("gx", "gy"),
        P("gx", "gy"),
        P("gx", "gy"),
        P(("gx", "gy"), None),
        P(("gx", "gy")),
        P(("gx", "gy"), None),
        P(("gx", "gy")),
        P(("gx", "gy"), None, None, None),
    )
    return jax.shard_map(
        functools.partial(shards, mesh.shape["gx"], mesh.shape["gy"]),
        mesh=mesh,
        in_specs=in_specs,
        out_specs=(P(None, "gx", "gy"), P("gx", "gy")),
        check_vma=False,
    )
```

time: 96.7 us -> 81.8 us (0.85)
  the two profiles are of different devices: /device:TPU:0 before, /device:TPU:1 now
where the time goes in v2:
time: 81.8 us; the launch traced here: 81.7 us
  Pallas kernels  78 us (95%)
  local copies, waits for them, and re-layouts  2.36 us (3%)
  between operations  1.3 us (2%)
    pallas_call x1, Pallas kernels, shards(): pl.pallas_call(functools.partial(body, n_gx, n_gy), out_shape=(jax.ShapeD...  78 us
    unnamed x4, local copies, waits for them, and re-layouts  2.36 us

profile of v2, /device:TPU:1, one launch (start us, length us, event | category | flops | bytes accessed | tf_op | source)
XLA Modules:
  0.0 81.7 jit_solution(11854371249778839011)
XLA Ops:
  1.3 78.0 %shelf.1 = (f32[2,128,256]{2,1,0:T(8,128)}, f32[128,256]{1,0:T(8,128)}) custom-call(s32[1]{0:T(128)S(6)} %copy.14.live_ref, s32[1,512]{1,0:T(1,128)} %bitcast.2, f32[1,512]{1,0:T(1,128)} %bitcast.3, f32[512,128]{1,0:T(8,128)} %misfit_hbm.1, f32[2,128,256]{2,1,0:T(8,128)} %start_hbm.1, f32[128,256]{1,0:T(8,128)} %visc_hbm.1, f32[128,256]{1,0:T(8,128)} %fric_hbm.1, ...), custom_call_target="tpu_custom_call" | custom-call | tf_op jit(solution)/shard_map/shelf/pallas_call | solution.py:395
  79.3 0.0 copy-start
  79.3 1.7 %copy.15 = f32[2,128,256]{2,1,0:T(8,128)} copy(f32[2,128,256]{2,1,0:T(8,128)} %get-tuple-element.4) | data formatting | bytes 524288
  81.0 0.0 copy-done
  81.0 0.7 copy.16
Async XLA Ops:
  79.3 1.7 %copy-start = (f32[128,256]{1,0:T(8,128)S(1)}, f32[128,256]{1,0:T(8,128)}, u32[]{:S(2)}) copy-start(f32[128,256]{1,0:T(8,128)} %get-tuple-element.5) | copy-start | bytes 393220

commit v3 on v2

--- a/solution.py
+++ b/solution.py
@@ -9,9 +9,12 @@
 
 ITERS = 4
 TAU = 0.04
+AHEAD = 6
 MESH = pl.DeviceIdType.MESH
 F32 = jnp.float32
 BF16 = jnp.bfloat16
+F8 = jnp.float8_e4m3fn
+PIECES = 3
 NT = (((1,), (1,)), ((), ()))
 NN = (((1,), (0,)), ((), ()))
 
@@ -60,21 +63,29 @@
 
 
 def scatter_group(rows8, cols8, values, acc_ref):
+    largest = functools.reduce(jnp.maximum, [jnp.abs(v) for pair in values for v in pair])
+    largest = jnp.maximum(jnp.max(largest, keepdims=True), 1e-30)
+    scale, back = 384.0 / largest, largest * (1.0 / 384.0)
     left, right = [], []
     sub = 16
     zero = jnp.zeros((sub, 128), BF16)
     unit = jnp.ones((sub, 128), BF16)
     for rows, cols, pair in zip(rows8, cols8, values):
+        pieces = []
+        for v in pair:
+            rest = v * scale
+            for _ in range(PIECES):
+                piece = rest.astype(BF16).astype(F8).astype(F32)
+                pieces.append(piece)
+                rest = (rest - piece) * 16.0
         for k in range(8):
             r = jnp.broadcast_to(rows[k : k + 1].astype(F32), (sub, 128)).astype(BF16)
             c = jnp.broadcast_to(cols[k : k + 1].astype(F32), (sub, 128)).astype(BF16)
-            pieces = []
-            for v in pair:
-                pieces += halves(jnp.broadcast_to(v[k : k + 1], (sub, 128)))
             at_row = hot(r, 128, sub)
-            left.append(jnp.concatenate([jnp.where(m, p, zero) for p in pieces for m in at_row], axis=0))
-            right.append(jnp.concatenate([jnp.where(m, unit, zero) for m in hot(c, 256, sub)], axis=0))
-    acc_ref[...] += mm(jnp.concatenate(left, axis=1), jnp.concatenate(right, axis=1), NT)
+            wide = [jnp.broadcast_to(p[k : k + 1], (sub, 128)).astype(BF16) for p in pieces]
+            left.append(jnp.concatenate([jnp.where(m, p, zero) for p in wide for m in at_row], axis=0).astype(F8))
+            right.append(jnp.concatenate([jnp.where(m, unit, zero) for m in hot(c, 256, sub)], axis=0).astype(F8))
+    acc_ref[...] += mm(jnp.concatenate(left, axis=1), jnp.concatenate(right, axis=1), NT) * back
 
 
 def neighbours(gx, gy, n_gx, n_gy):
@@ -134,9 +145,11 @@
     for i, field in enumerate(fields):
         sub = lax.broadcasted_iota(jnp.int32, (8, 256), 0) < 4
         ext[field, 128:136, 0:256] = jnp.where(sub, has(bottom, rows[0, i]), has(top, rows[1, i]))
-        lane = lax.broadcasted_iota(jnp.int32, (128, 128), 1)
-        value = jnp.where(lane < 64, has(east, cols[0, i]), has(west, cols[1, i]))
-        ext[field, 0:128, 256:384] = jnp.where((lane < 4) | (lane >= 124), value, 0.0)
+        sub = lax.broadcasted_iota(jnp.int32, (8, 128), 0) < 4
+        first = jnp.where(sub, has(east, cols[0, i]), 0.0)
+        last = jnp.where(sub, 0.0, has(west, cols[1, i]))
+        turned = jnp.concatenate([first, jnp.zeros((112, 128), F32), last], axis=0)
+        ext[field, 0:128, 256:384] = turned.T
         lane = lax.broadcasted_iota(jnp.int32, (8, 128), 1)
         sub = lax.broadcasted_iota(jnp.int32, (8, 128), 0) < 4
         below = jnp.where(lane < 64, has(both(bottom, east), corners[0, i]), has(both(bottom, west), corners[1, i]))
@@ -172,9 +185,11 @@
 def pack_edge(i, field, packed):
     rows, cols, corner = packed
     rows[i] = pack_rows(field)
-    cols[i] = pack_cols(field)
+    edge = pack_cols(field)
+    turned = edge.T
     first = lax.broadcasted_iota(jnp.int32, (8, 128), 0) < 4
-    corner[i] = jnp.where(first, cols[i, 0:8], cols[i, 120:128])
+    cols[i] = jnp.where(first, turned[0:8], turned[120:128])
+    corner[i] = jnp.where(first, edge[0:8], edge[120:128])
 
 
 def body(
@@ -188,10 +203,8 @@
     visc_hbm,
     fric_hbm,
     mask_hbm,
-    vel_hbm,
     lists_hbm,
-    adj_ref,
-    grad_ref,
+    ice_ref,
     dest_ref,
     heading_ref,
     misfit_ref,
@@ -199,7 +212,6 @@
     visc_ref,
     fric_ref,
     mask_ref,
-    vel_ref,
     lists,
     outgoing,
     arrived,
@@ -239,7 +251,6 @@
                 (fric_hbm, fric_ref),
                 (mask_hbm, mask_ref),
                 (lists_hbm, lists),
-                (vel_hbm, vel_ref),
             ]
         )
     ]
@@ -265,14 +276,8 @@
         pack_edge(i, f, fixed_packed)
 
     pl.semaphore_wait(barrier, n_gx + n_gy - 2)
-    for b in range(1, n_gy):
-        pl.semaphore_signal(all_sem, inc=1, device_id=(gx, lax.rem(gy + b, n_gy)), device_id_type=MESH)
-    pl.semaphore_wait(all_sem, n_gy - 1)
-
     fixed_got = (fixed_got_rows, fixed_got_cols, fixed_got_corners)
     fixed_copies = edge_copies(around, fixed_packed, fixed_got, fixed_sems)
-    for copy in fixed_copies:
-        copy.start()
 
     def send_group(g, first=0):
         y = lax.rem(gy + g, n_gy)
@@ -289,7 +294,55 @@
 
     pltpu.make_async_copy(outgoing.at[me], arrived.at[gy, gx], recv_sem.at[0]).start()
     send_group(0, 1)
-    send_group(1)
+    for b in range(1, n_gy):
+        pl.semaphore_signal(
+            all_sem.at[b], inc=1, device_id=(gx, lax.rem(gy + n_gy - b, n_gy)), device_id_type=MESH
+        )
+
+    def send_next(g, carry):
+        pl.semaphore_wait(all_sem.at[g], 1)
+        send_group(g)
+        return carry
+
+    lax.fori_loop(1, AHEAD, send_next, 0)
+    for copy in loads[7:8]:
+        copy.wait()
+
+    def take_group(g):
+        y = lax.rem(gy + n_gy - g, n_gy)
+        pltpu.make_async_copy(outgoing.at[0:n_gx], arrived.at[y], recv_sem.at[g]).wait()
+        sources = [x * n_gy + y for x in range(n_gx)]
+        scatter_group(
+            [lists[s, :, 0, :] for s in sources],
+            [lists[s, :, 1, :] for s in sources],
+            [(arrived[y, x, 0:8, :], arrived[y, x, 8:16, :]) for x in range(n_gx)],
+            acc,
+        )
+
+    def send_and_take(g, carry):
+        send_next(g + AHEAD, carry)
+        take_group(g)
+        return carry
+
+    def take(g, carry):
+        take_group(g)
+        return carry
+
+    lax.fori_loop(0, n_gy - AHEAD, send_and_take, 0)
+    for copy in fixed_copies:
+        copy.start()
+    lax.fori_loop(n_gy - AHEAD, n_gy, take, 0)
+
+    load_packed = (load_rows, load_cols, load_corner)
+    for i in range(2):
+        parts = [acc[128 * (PIECES * i + p) : 128 * (PIECES * i + p + 1)] for p in range(PIECES)]
+        f = parts[0] + (parts[1] + parts[2] * (1.0 / 16.0)) * (1.0 / 16.0)
+        ext[i, 0:128, 0:256] = f
+        pack_edge(i, f, load_packed)
+    load_got = (load_got_rows, load_got_cols, load_got_corners)
+    load_copies = edge_copies(around, load_packed, load_got, load_sems)
+    for copy in load_copies:
+        copy.start()
 
     for copy in fixed_copies:
         copy.wait_recv()
@@ -303,41 +356,7 @@
     out_e, out_n = apply(ext[2], ext[3], ext[4], ext[7], ext[8], ext[5])
     ext[2] = ext[2] - ext[9] * out_e
     ext[3] = ext[3] - ext[9] * out_n
-    for copy in loads[7:9]:
-        copy.wait()
-
-    def take_group(g):
-        y = lax.rem(gy + n_gy - g, n_gy)
-        pltpu.make_async_copy(outgoing.at[0:n_gx], arrived.at[y], recv_sem.at[g]).wait()
-        sources = [x * n_gy + y for x in range(n_gx)]
-        scatter_group(
-            [lists[s, :, 0, :] for s in sources],
-            [lists[s, :, 1, :] for s in sources],
-            [(arrived[y, x, 0:8, :], arrived[y, x, 8:16, :]) for x in range(n_gx)],
-            acc,
-        )
-
-    def send_and_take(g, carry):
-        send_group(g + 2)
-        take_group(g)
-        return carry
-
-    def take(g, carry):
-        take_group(g)
-        return carry
-
-    lax.fori_loop(0, n_gy - 2, send_and_take, 0)
-    lax.fori_loop(n_gy - 2, n_gy, take, 0)
-
-    load_packed = (load_rows, load_cols, load_corner)
-    for i in range(2):
-        f = acc[256 * i : 256 * i + 128] + acc[256 * i + 128 : 256 * i + 256]
-        ext[i, 0:128, 0:256] = f
-        pack_edge(i, f, load_packed)
-    load_got = (load_got_rows, load_got_cols, load_got_corners)
-    load_copies = edge_copies(around, load_packed, load_got, load_sems)
-    for copy in load_copies:
-        copy.start()
+
     for copy in load_copies:
         copy.wait_recv()
     fill_edges(ext, range(2), flags, *load_got)
@@ -353,12 +372,7 @@
         return carry
 
     lax.fori_loop(0, ITERS - 1, sweep, 0)
-    on_ice = mask_ref[...] > 0
-    keep = (1.0 - TAU) ** ITERS
-    w_e, w_n = ext[2, 0:128, 0:256], ext[3, 0:128, 0:256]
-    adj_ref[0] = jnp.where(on_ice, w_e, keep * start_ref[0])
-    adj_ref[1] = jnp.where(on_ice, w_n, keep * start_ref[1])
-    grad_ref[...] = -(fric_ref[...] * (vel_ref[0] * w_e + vel_ref[1] * w_n))
+    ice_ref[...] = ext[2:4, 0:128, 0:256]
 
     for copy in fixed_copies + load_copies:
         copy.wait_send()
@@ -373,6 +387,14 @@
     ).wait_send()
 
 
+def finish(ice_ref, start_ref, fric_ref, mask_ref, vel_ref, adj_ref, grad_ref):
+    here = mask_ref[...] > 0
+    keep = (1.0 - TAU) ** ITERS
+    adj_ref[0] = jnp.where(here, ice_ref[0], keep * start_ref[0])
+    adj_ref[1] = jnp.where(here, ice_ref[1], keep * start_ref[1])
+    grad_ref[...] = -(fric_ref[...] * (vel_ref[0] * ice_ref[0] + vel_ref[1] * ice_ref[1]))
+
+
 VMEM = pl.BlockSpec(memory_space=pltpu.VMEM)
 SMEM = pl.BlockSpec(memory_space=pltpu.SMEM)
 HBM = pl.BlockSpec(memory_space=pltpu.HBM)
@@ -381,10 +403,10 @@
 def edge_scratch(fields):
     return [
         pltpu.VMEM((fields, 8, 256), F32),
-        pltpu.VMEM((fields, 128, 128), F32),
+        pltpu.VMEM((fields, 8, 128), F32),
         pltpu.VMEM((fields, 8, 128), F32),
         pltpu.VMEM((2, fields, 8, 256), F32),
-        pltpu.VMEM((2, fields, 128, 128), F32),
+        pltpu.VMEM((2, fields, 8, 128), F32),
         pltpu.VMEM((4, fields, 8, 128), F32),
     ]
 
@@ -392,11 +414,11 @@
 def shards(n_gx, n_gy, start, velocity, viscosity, friction, ice_mask, misfit, heading, row_dest, live_rows, lists):
     tiles = n_gx * n_gy
     own = misfit.shape[0]
-    return pl.pallas_call(
+    on_ice = pl.pallas_call(
         functools.partial(body, n_gx, n_gy),
-        out_shape=(jax.ShapeDtypeStruct((2, 128, 256), F32), jax.ShapeDtypeStruct((128, 256), F32)),
-        in_specs=[SMEM] + [HBM] * 9,
-        out_specs=(VMEM, VMEM),
+        out_shape=jax.ShapeDtypeStruct((2, 128, 256), F32),
+        in_specs=[SMEM] + [HBM] * 8,
+        out_specs=VMEM,
         scratch_shapes=[
             pltpu.VMEM((1, own), jnp.int32),
             pltpu.VMEM((1, own), F32),
@@ -405,20 +427,19 @@
             pltpu.VMEM(viscosity.shape, F32),
             pltpu.VMEM(friction.shape, F32),
             pltpu.VMEM(ice_mask.shape, jnp.int32),
-            pltpu.VMEM(velocity.shape, F32),
             pltpu.VMEM(lists.shape, jnp.int32),
             pltpu.VMEM((tiles, 16, 128), F32),
             pltpu.VMEM((n_gy, n_gx, 16, 128), F32),
-            pltpu.VMEM((512, 256), F32),
+            pltpu.VMEM((2 * PIECES * 128, 256), F32),
             pltpu.VMEM((10, 136, 384), F32),
             *edge_scratch(5),
             *edge_scratch(2),
-            pltpu.SemaphoreType.DMA((9,)),
+            pltpu.SemaphoreType.DMA((8,)),
             pltpu.SemaphoreType.DMA,
             pltpu.SemaphoreType.DMA((n_gy,)),
             pltpu.SemaphoreType.DMA((2, 8)),
             pltpu.SemaphoreType.DMA((2, 8)),
-            pltpu.SemaphoreType.REGULAR,
+            pltpu.SemaphoreType.REGULAR((n_gy,)),
         ],
         compiler_params=pltpu.CompilerParams(collective_id=0, has_side_effects=True, vmem_limit_bytes=60 << 20),
         name="shelf",
@@ -431,9 +452,15 @@
         viscosity,
         friction,
         ice_mask,
-        velocity,
         lists,
     )
+    return pl.pallas_call(
+        finish,
+        out_shape=(jax.ShapeDtypeStruct((2, 128, 256), F32), jax.ShapeDtypeStruct((128, 256), F32)),
+        in_specs=[VMEM] * 5,
+        out_specs=(VMEM, VMEM),
+        name="finish",
+    )(on_ice, start, friction, ice_mask, velocity)
 
 
 def solution(mesh):

time: 81.8 us -> 59.4 us (0.73)
  the two profiles are of different devices: /device:TPU:1 before, /device:TPU:3 now
where the time goes in v3:
time: 59.4 us; the launch traced here: 59.3 us
  Pallas kernels  58 us (98%)
  between operations  1.29 us (2%)
    pallas_call x1, Pallas kernels, shards(): pl.pallas_call(functools.partial(body, n_gx, n_gy), out_shape=jax.ShapeDt...  56 us
    pallas_call x1, Pallas kernels, shards(): pl.pallas_call(finish, out_shape=(jax.ShapeDtypeStruct((2, 128, 256), F32...  2 us

profile of v3, /device:TPU:3, one launch (start us, length us, event | category | flops | bytes accessed | tf_op | source)
XLA Modules:
  0.0 59.3 jit_solution(13673068836760640905)
XLA Ops:
  1.3 56.0 %shelf.1.ice_ref = f32[2,128,256]{2,1,0:T(8,128)} custom-call(s32[1]{0:T(128)S(6)} %copy.12.live_ref, s32[1,512]{1,0:T(1,128)} %bitcast.2, f32[1,512]{1,0:T(1,128)} %bitcast.3, f32[512,128]{1,0:T(8,128)} %misfit_hbm.1, f32[2,128,256]{2,1,0:T(8,128)} %start_ref.1, f32[128,256]{1,0:T(8,128)} %visc_hbm.1, f32[128,256]{1,0:T(8,128)} %fric_ref.1, ...), custom_call_target="tpu_custom_call" | custom-call | tf_op jit(solution)/shard_map/shelf/pallas_call | solution.py:417
  57.3 2.0 %finish.1 = (f32[2,128,256]{2,1,0:T(8,128)}, f32[128,256]{1,0:T(8,128)}) custom-call(f32[2,128,256]{2,1,0:T(8,128)} %shelf.1.ice_ref, f32[2,128,256]{2,1,0:T(8,128)} %start_ref.1, f32[128,256]{1,0:T(8,128)} %fric_ref.1, s32[128,256]{1,0:T(8,128)} %mask_ref.1, f32[2,128,256]{2,1,0:T(8,128)} %vel_ref.1), custom_call_target="tpu_custom_call" | custom-call | tf_op jit(solution)/shard_map/finish/pallas_call | solution.py:457

commit v4 on v3

--- a/solution.py
+++ b/solution.py
@@ -268,12 +268,6 @@
     route(live_ref, dest_ref, heading_ref, misfit_ref, outgoing)
     acc[...] = jnp.zeros_like(acc)
     fixed_packed = (fixed_rows, fixed_cols, fixed_corner)
-    for copy in loads[3:7]:
-        copy.wait()
-    fields = [start_ref[0], start_ref[1], visc_ref[...], fric_ref[...], mask_ref[...].astype(F32)]
-    for i, f in enumerate(fields):
-        ext[2 + i, 0:128, 0:256] = f
-        pack_edge(i, f, fixed_packed)
 
     pl.semaphore_wait(barrier, n_gx + n_gy - 2)
     fixed_got = (fixed_got_rows, fixed_got_cols, fixed_got_corners)
@@ -305,6 +299,12 @@
         return carry
 
     lax.fori_loop(1, AHEAD, send_next, 0)
+    for copy in loads[3:7]:
+        copy.wait()
+    fields = [start_ref[0], start_ref[1], visc_ref[...], fric_ref[...], mask_ref[...].astype(F32)]
+    for i, f in enumerate(fields):
+        ext[2 + i, 0:128, 0:256] = f
+        pack_edge(i, f, fixed_packed)
     for copy in loads[7:8]:
         copy.wait()
 
@@ -387,12 +387,28 @@
     ).wait_send()
 
 
-def finish(ice_ref, start_ref, fric_ref, mask_ref, vel_ref, adj_ref, grad_ref):
+def finish(
+    ice_hbm, start_hbm, fric_hbm, mask_hbm, vel_hbm, adj_hbm, grad_hbm, ice_ref, start_ref, fric_ref, mask_ref, vel_ref, adj_ref, grad_ref, sems
+):
+    pairs = [(ice_hbm, ice_ref), (start_hbm, start_ref), (mask_hbm, mask_ref), (fric_hbm, fric_ref), (vel_hbm, vel_ref)]
+    loads = [pltpu.make_async_copy(src, dst, sems.at[i]) for i, (src, dst) in enumerate(pairs)]
+    for copy in loads:
+        copy.start()
+    for copy in loads[0:3]:
+        copy.wait()
     here = mask_ref[...] > 0
     keep = (1.0 - TAU) ** ITERS
     adj_ref[0] = jnp.where(here, ice_ref[0], keep * start_ref[0])
     adj_ref[1] = jnp.where(here, ice_ref[1], keep * start_ref[1])
+    adj_copy = pltpu.make_async_copy(adj_ref, adj_hbm, sems.at[5])
+    adj_copy.start()
+    for copy in loads[3:5]:
+        copy.wait()
     grad_ref[...] = -(fric_ref[...] * (vel_ref[0] * ice_ref[0] + vel_ref[1] * ice_ref[1]))
+    grad_copy = pltpu.make_async_copy(grad_ref, grad_hbm, sems.at[6])
+    grad_copy.start()
+    adj_copy.wait()
+    grad_copy.wait()
 
 
 VMEM = pl.BlockSpec(memory_space=pltpu.VMEM)
@@ -457,8 +473,19 @@
     return pl.pallas_call(
         finish,
         out_shape=(jax.ShapeDtypeStruct((2, 128, 256), F32), jax.ShapeDtypeStruct((128, 256), F32)),
-        in_specs=[VMEM] * 5,
-        out_specs=(VMEM, VMEM),
+        in_specs=[HBM] * 5,
+        out_specs=(HBM, HBM),
+        scratch_shapes=[
+            pltpu.VMEM((2, 128, 256), F32),
+            pltpu.VMEM((2, 128, 256), F32),
+            pltpu.VMEM((128, 256), F32),
+            pltpu.VMEM((128, 256), jnp.int32),
+            pltpu.VMEM((2, 128, 256), F32),
+            pltpu.VMEM((2, 128, 256), F32),
+            pltpu.VMEM((128, 256), F32),
+            pltpu.SemaphoreType.DMA((7,)),
+        ],
+        compiler_params=pltpu.CompilerParams(vmem_limit_bytes=60 << 20),
         name="finish",
     )(on_ice, start, friction, ice_mask, velocity)
 

time: 59.4 us -> 59.5 us (level)
  no operation moved by 1% of the time
where the time goes in v4:
time: 59.5 us; the launch traced here: 59.3 us
  Pallas kernels  58 us (97%)
  between operations  1.29 us (2%)
    pallas_call x1, Pallas kernels, shards(): pl.pallas_call(functools.partial(body, n_gx, n_gy), out_shape=jax.ShapeDt...  56.1 us
    pallas_call x1, Pallas kernels, shards(): pl.pallas_call(finish, out_shape=(jax.ShapeDtypeStruct((2, 128, 256), F32...  1.94 us

profile of v4, /device:TPU:3, one launch (start us, length us, event | category | flops | bytes accessed | tf_op | source)
XLA Modules:
  0.0 59.3 jit_solution(16593281435232398737)
XLA Ops:
  1.3 56.1 %shelf.1.ice_hbm = f32[2,128,256]{2,1,0:T(8,128)} custom-call(s32[1]{0:T(128)S(6)} %copy.12.live_ref, s32[1,512]{1,0:T(1,128)} %bitcast.2, f32[1,512]{1,0:T(1,128)} %bitcast.3, f32[512,128]{1,0:T(8,128)} %misfit_hbm.1, f32[2,128,256]{2,1,0:T(8,128)} %start_hbm.3, f32[128,256]{1,0:T(8,128)} %visc_hbm.1, f32[128,256]{1,0:T(8,128)} %fric_hbm.3, ...), custom_call_target="tpu_custom_call" | custom-call | tf_op jit(solution)/shard_map/shelf/pallas_call | solution.py:433
  57.4 1.9 %finish.1 = (f32[2,128,256]{2,1,0:T(8,128)}, f32[128,256]{1,0:T(8,128)}) custom-call(f32[2,128,256]{2,1,0:T(8,128)} %shelf.1.ice_hbm, f32[2,128,256]{2,1,0:T(8,128)} %start_hbm.3, f32[128,256]{1,0:T(8,128)} %fric_hbm.3, s32[128,256]{1,0:T(8,128)} %mask_hbm.3, f32[2,128,256]{2,1,0:T(8,128)} %vel_hbm.1), custom_call_target="tpu_custom_call" | custom-call | tf_op jit(solution)/shard_map/finish/pallas_call | solution.py:473
